TPU v7x, 256 devices: a whole 4x4x8 slice. The times are simulated.
256 devices in a mesh: row: 16 (over z, y_lo), col: 16 (over y_hi, x, core).
Axes of the slice: x: 4, y: 4 (y_hi: 2, y_lo: 2; y = y_hi * 2 + y_lo), z: 8, core: 2. Of those that a mesh axis runs over, the one named last changes fastest.
Arguments:
- features: float32 [32, 24576], P(None, ('row', 'col')), may hold values from -6 to 6
- block: float32 [16, 24576], P(None, ('row', 'col')), may hold values from -6 to 6
Outputs:
- applied: float32 [16, 24576], P(None, ('row', 'col'))
All inputs are finite; a program needn't handle non-finite values.
Results may differ from a plain program's by a relative error of at most 0.006.
Values may be sent and summed in bfloat16 or wider, within the bound.
No kernel may reach another device: no remote copies, remote signals or barrier semaphores. Data moves between devices by JAX's collectives and lax.ppermute only.
A program may use at most 64 MiB of HBM per device.

v0:
```python
import math

import jax
import jax.numpy as jnp
from jax import lax
from jax.sharding import PartitionSpec as P


def split_up(x, dim, count):
    shape = x.shape
    parts = x.reshape(*shape[:dim], count, shape[dim] // count, *shape[dim + 1 :])
    return jnp.moveaxis(parts, dim, 0)


def sent_and_summed(x, axis, dim):
    parts = split_up(x, dim, lax.axis_size(axis))
    arrived = lax.all_to_all(parts, axis, split_axis=0, concat_axis=0, tiled=True)
    return arrived.sum(axis=0)


def laid_out(parts, dim):
    parts = jnp.moveaxis(parts, 0, dim)
    shape = parts.shape
    return parts.reshape(*shape[:dim], shape[dim] * shape[dim + 1], *shape[dim + 2 :])


def sent_to_all(x, axis):
    copies = jnp.broadcast_to(x, (lax.axis_size(axis), *x.shape))
    return lax.all_to_all(copies, axis, split_axis=0, concat_axis=0, tiled=True)


def collect(x, axis, dim):
    return laid_out(sent_to_all(x, axis), dim)


def taken_together(x, axis):
    everything = sent_to_all(x, axis)
    return jnp.sum(everything, axis=0)


def kernel_rows(row_feat, row_sq, col_feat, col_sq, scale, start, count):
    part = lax.dynamic_slice_in_dim(row_feat, start, count, 1)
    sq_part = lax.dynamic_slice_in_dim(row_sq, start, count, 0)
    inner = jnp.einsum("fi,fj->ij", part, col_feat, precision=lax.Precision.HIGHEST)
    dist = sq_part[:, None] + col_sq[None, :] - 2.0 * inner
    return jnp.exp(-dist / scale).astype(jnp.bfloat16)


def combine(partial_value):
    return sent_and_summed(partial_value, "col", 1)


def full_plan(features, block, row_feat, scale):
    col_feat = collect(features, "row", 1)
    row_sq = jnp.sum(row_feat * row_feat, axis=0)
    col_sq = jnp.sum(col_feat * col_feat, axis=0)
    rows = row_feat.shape[1]
    step = math.gcd(512, rows)
    count_blocks = rows // step
    starts = jnp.arange(count_blocks, dtype=jnp.int32) * step
    indexes = jnp.arange(count_blocks, dtype=jnp.int32)

    def fetch(index):
        return kernel_rows(row_feat, row_sq, col_feat, col_sq, scale, starts[index], step)

    def first_pass(index):
        tile = fetch(index)
        return (jnp.sum(tile, axis=1, dtype=jnp.float32), jnp.sum(tile, axis=0, dtype=jnp.float32))

    row_parts, col_parts = lax.map(first_pass, indexes)
    q_own = combine(row_parts.reshape(1, rows))
    inv_own = 1.0 / q_own
    col_total = taken_together(jnp.sum(col_parts, axis=0)[None, :], "row")
    inv_col = 1.0 / col_total

    def second_pass(index):
        return jnp.sum(fetch(index).astype(jnp.float32) * inv_col, axis=1)

    second = combine(lax.map(second_pass, indexes).reshape(1, rows))
    dens = second * inv_own
    factor = inv_own * lax.rsqrt(dens)
    weighted = (block * factor).astype(jnp.bfloat16)
    weighted_col = collect(weighted, "row", 1)

    def third_pass(index):
        return jnp.einsum(
            "kj,ij->ki", weighted_col, fetch(index), preferred_element_type=jnp.float32
        )

    products = lax.map(third_pass, indexes)
    partial_value = jnp.moveaxis(products, 0, 1).reshape(block.shape[0], rows)
    return combine(partial_value) * factor


def per_device(features, block):
    n_row = lax.axis_size("row")
    n_col = lax.axis_size("col")
    width, owned = features.shape
    frames = owned * n_row * n_col
    scale = 4.0 / (float(frames) ** (2.0 / width) - 1.0)
    row_feat = collect(features, "col", 1)
    return full_plan(features, block, row_feat, scale)


def solution(mesh):
    placed = (P(None, ("row", "col")), P(None, ("row", "col")))
    return jax.shard_map(
        per_device, mesh=mesh, in_specs=placed, out_specs=P(None, ("row", "col")), check_vma=False
    )
```

profile of v0, /device:TPU:1, one launch (start us, length us, event | category | flops | bytes accessed | tf_op | source)
XLA Modules:
  0.0 182.2 jit_solution(8991631559053315384)
XLA Ops:
  0.0 1.4 broadcast_in_dim.39
  1.4 17.1 %all_to_all.35 = f32[16,32,96]{2,1,0:T(8,128)S(1)} all-to-all(f32[16,32,96]{2,1,0:T(8,128)} %broadcast_in_dim.39), channel_id=1, replica_groups=mesh['row'=16,'col'=16] {'col'}, dimensions={0} | all-to-all | bytes 393216 | tf_op jit(solution)/shard_map/all_to_all | solution.py:29
  18.6 8.4 %all-to-all-start.1 = ((f32[16,32,96]{2,1,0:T(8,128)}), f32[16,32,96]{2,1,0:T(8,128)S(1)}, u32[]{:S(2)}, u32[]{:S(2)}) async-start(f32[16,32,96]{2,1,0:T(8,128)} %broadcast_in_dim.39), calls=%async_computation.1 | async-start | bytes 524288 | tf_op jit(solution)/shard_map/all_to_all | solution.py:29
  27.4 9.7 %all-to-all-done.1 = f32[16,32,96]{2,1,0:T(8,128)S(1)} async-done(((f32[16,32,96]{2,1,0:T(8,128)}), f32[16,32,96]{2,1,0:T(8,128)S(1)}, u32[]{:S(2)}, u32[]{:S(2)}) %all-to-all-start.1) | async-done | bytes 196640 | tf_op jit(solution)/shard_map/all_to_all | solution.py:29
  37.5 28.3 %while.32 = (s32[]{:T(128)}, f32[3,512]{1,0:T(4,128)S(1)}, f32[3,1536]{1,0:T(4,128)S(1)}, s32[3]{0:T(128)S(1)}, s32[3]{0:T(128)S(1)}, /*index=5*/f32[1536]{0:T(1...) while((s32[]{:T(128)}, f32[3,512]{1,0:T(4,128)S(1)}, ...), condition=%wide.region_5.6_spmd, body=%wide.region_2.5_spmd.sunk | while | flops 309065728 | bytes 313577 | solution.py:70
  37.5 0.7 dynamic_slice.58
  40.3 0.7 dynamic_slice.59
  43.1 3.7 %convert_reduce_fusion.3 = (f32[1536]{0:T(1024)S(1)}, f32[512]{0:T(512)S(1)}) fusion(f32[32,1536]{1,0:T(8,128)S(1)} %get-tuple-element.410, f32[32,1536]{1,0:T(8,128)S(1)} %get-tuple-element.409, s32[]{:T(128)S(6)} %select_n.28, f32[1536]{0:T(1024)S(1)} %get-tuple-element.408, f32[512]{0:T(512)S(1)} %dynamic_slice.60), kind=kOutput, calls=%fused_computation.clone.1 | convolution fusion | flops 309065728 | bytes 280580 | tf_op jit(solution)/shard_map/while/body/eval_jaxpr/fi,fj->ij/dot_general | solution.py:44
  47.0 0.7 dynamic_slice.58
  49.7 0.7 dynamic_slice.59
  52.5 3.7 %convert_reduce_fusion.3 = (f32[1536]{0:T(1024)S(1)}, f32[512]{0:T(512)S(1)}) fusion(f32[32,1536]{1,0:T(8,128)S(1)} %get-tuple-element.410, f32[32,1536]{1,0:T(8,128)S(1)} %get-tuple-element.409, s32[]{:T(128)S(6)} %select_n.28, f32[1536]{0:T(1024)S(1)} %get-tuple-element.408, f32[512]{0:T(512)S(1)} %dynamic_slice.60), kind=kOutput, calls=%fused_computation.clone.1 | convolution fusion | flops 309065728 | bytes 280580 | tf_op jit(solution)/shard_map/while/body/eval_jaxpr/fi,fj->ij/dot_general | solution.py:44
  56.4 0.7 dynamic_slice.58
  59.1 0.7 dynamic_slice.59
  62.0 3.7 %convert_reduce_fusion.3 = (f32[1536]{0:T(1024)S(1)}, f32[512]{0:T(512)S(1)}) fusion(f32[32,1536]{1,0:T(8,128)S(1)} %get-tuple-element.410, f32[32,1536]{1,0:T(8,128)S(1)} %get-tuple-element.409, s32[]{:T(128)S(6)} %select_n.28, f32[1536]{0:T(1024)S(1)} %get-tuple-element.408, f32[512]{0:T(512)S(1)} %dynamic_slice.60), kind=kOutput, calls=%fused_computation.clone.1 | convolution fusion | flops 309065728 | bytes 280580 | tf_op jit(solution)/shard_map/while/body/eval_jaxpr/fi,fj->ij/dot_general | solution.py:44
  65.9 0.7 broadcast_in_dim.41
  66.5 3.6 %all-to-all-start.3 = ((f32[16,1,1536]{2,1,0:T(1,128)}), f32[16,1,1536]{2,1,0:T(1,128)S(1)}, u32[]{:S(2)}, u32[]{:S(2)}) async-start(f32[16,1,1536]{2,1,0:T(1,128)} %broadcast_in_dim.41), calls=%async_computation.3 | async-start | bytes 196608 | tf_op jit(solution)/shard_map/all_to_all | solution.py:29
  70.1 0.7 transpose_reshape_reshape.6
  70.8 7.6 %all-to-all-done.3 = f32[16,1,1536]{2,1,0:T(1,128)S(1)} async-done(((f32[16,1,1536]{2,1,0:T(1,128)}), f32[16,1,1536]{2,1,0:T(1,128)S(1)}, u32[]{:S(2)}, u32[]{:S(2)}) %all-to-all-start.3) | async-done | bytes 98336 | tf_op jit(solution)/shard_map/all_to_all | solution.py:29
  78.4 7.4 %all-to-all-start.2 = ((f32[16,1,96]{2,1,0:T(1,128)}), f32[16,1,96]{2,1,0:T(1,128)S(1)}, u32[]{:S(2)}, u32[]{:S(2)}) async-start(f32[16,1,96]{2,1,0:T(1,128)} %transpose_reshape_reshape.6), calls=%async_computation.2 | async-start | bytes 16384 | tf_op jit(solution)/shard_map/all_to_all | solution.py:17
  86.0 28.0 %while.33 = (s32[]{:T(128)}, f32[3,512]{1,0:T(4,128)S(1)}, s32[3]{0:T(128)S(1)}, s32[3]{0:T(128)S(1)}, f32[1536]{0:T(1024)S(1)}, /*index=5*/f32[1536]{0:T(1024)S...) while((s32[]{:T(128)}, f32[3,512]{1,0:T(4,128)S(1)}, ...), condition=%wide.region_11.12_spmd, body=%wide.region_9.11_spmd.sunk | while | flops 309067264 | bytes 303345 | solution.py:79
  86.0 0.7 dynamic_slice.62
  88.7 0.7 dynamic_slice.63
  91.6 3.7 %multiply_reduce_fusion.4 = f32[512]{0:T(512)S(1)} fusion(f32[1536]{0:T(1024)S(1)} %reduce.7, f32[32,1536]{1,0:T(8,128)S(1)} %get-tuple-element.450, f32[1536]{0:T(1024)S(1)} %get-tuple-element.448, f32[512]{0:T(512)S(1)} %dynamic_slice.64, f32[32,1536]{1,0:T(8,128)S(1)} %get-tuple-element.449, s32[]{:T(128)S(6)} %select_n.30), kind=kOutput, calls=%fused_computation.25.clone.1 | convolution fusion | flops 309067264 | bytes 282628 | tf_op jit(solution)/shard_map/while/body/eval_jaxpr/fi,fj->ij/dot_general | solution.py:44
  95.3 0.7 dynamic_slice.62
  98.0 0.7 dynamic_slice.63
  100.9 3.7 %multiply_reduce_fusion.4 = f32[512]{0:T(512)S(1)} fusion(f32[1536]{0:T(1024)S(1)} %reduce.7, f32[32,1536]{1,0:T(8,128)S(1)} %get-tuple-element.450, f32[1536]{0:T(1024)S(1)} %get-tuple-element.448, f32[512]{0:T(512)S(1)} %dynamic_slice.64, f32[32,1536]{1,0:T(8,128)S(1)} %get-tuple-element.449, s32[]{:T(128)S(6)} %select_n.30), kind=kOutput, calls=%fused_computation.25.clone.1 | convolution fusion | flops 309067264 | bytes 282628 | tf_op jit(solution)/shard_map/while/body/eval_jaxpr/fi,fj->ij/dot_general | solution.py:44
  104.6 0.7 dynamic_slice.62
  107.4 0.7 dynamic_slice.63
  110.2 3.7 %multiply_reduce_fusion.4 = f32[512]{0:T(512)S(1)} fusion(f32[1536]{0:T(1024)S(1)} %reduce.7, f32[32,1536]{1,0:T(8,128)S(1)} %get-tuple-element.450, f32[1536]{0:T(1024)S(1)} %get-tuple-element.448, f32[512]{0:T(512)S(1)} %dynamic_slice.64, f32[32,1536]{1,0:T(8,128)S(1)} %get-tuple-element.449, s32[]{:T(128)S(6)} %select_n.30), kind=kOutput, calls=%fused_computation.25.clone.1 | convolution fusion | flops 309067264 | bytes 282628 | tf_op jit(solution)/shard_map/while/body/eval_jaxpr/fi,fj->ij/dot_general | solution.py:44
  113.9 0.7 transpose_reshape_reshape.7
  114.6 7.2 %all-to-all-start.4 = ((f32[16,1,96]{2,1,0:T(1,128)}), f32[16,1,96]{2,1,0:T(1,128)S(1)}, u32[]{:S(2)}, u32[]{:S(2)}) async-start(f32[16,1,96]{2,1,0:T(1,128)} %transpose_reshape_reshape.7), calls=%async_computation.4 | async-start | bytes 16384 | tf_op jit(solution)/shard_map/all_to_all | solution.py:17
  121.9 6.9 %all-to-all-done.4 = f32[16,1,96]{2,1,0:T(1,128)S(1)} async-done(((f32[16,1,96]{2,1,0:T(1,128)}), f32[16,1,96]{2,1,0:T(1,128)S(1)}, u32[]{:S(2)}, u32[]{:S(2)}) %all-to-all-start.4) | async-done | bytes 6176 | tf_op jit(solution)/shard_map/all_to_all | solution.py:17
  128.8 0.6 broadcast_in_dim.42
  129.5 3.7 %all-to-all-start.5 = ((bf16[16,16,96]{2,1,0:T(8,128)(2,1)}), bf16[16,16,96]{2,1,0:T(8,128)(2,1)S(1)}, u32[]{:S(2)}, u32[]{:S(2)}) async-start(bf16[16,16,96]{2,1,0:T(8,128)(2,1)} %broadcast_in_dim.42), calls=%async_computation.5 | async-start | bytes 131072 | tf_op jit(solution)/shard_map/all_to_all | solution.py:29
  133.2 7.7 %all-to-all-done.5 = bf16[16,16,96]{2,1,0:T(8,128)(2,1)S(1)} async-done(((bf16[16,16,96]{2,1,0:T(8,128)(2,1)}), bf16[16,16,96]{2,1,0:T(8,128)(2,1)S(1)}, u32[]{:S(2)}, u32[]{:S(2)}) %all-to-all-start.5) | async-done | bytes 49184 | tf_op jit(solution)/shard_map/all_to_all | solution.py:29
  141.0 28.4 %while.34 = (s32[]{:T(128)}, f32[3,16,512]{2,1,0:T(8,128)S(1)}, s32[3]{0:T(128)S(1)}, s32[3]{0:T(128)S(1)}, f32[1536]{0:T(1024)S(1)}, /*index=5*/f32[1536]{0:T(1...) while((s32[]{:T(128)}, f32[3,16,512]{2,1,0:T(8,128)S(1)}, ...), condition=%wide.region_14.15_spmd, body=%wide.region_13.14_spmd.sunk | while | flops 331874304 | bytes 3504357 | solution.py:90
  141.0 0.7 dynamic_slice.66
  143.8 0.7 dynamic_slice.67
  146.6 3.4 %fusion.43 = bf16[512,1536]{1,0:T(8,128)(2,1)S(1)} fusion(f32[32,1536]{1,0:T(8,128)S(1)} %get-tuple-element.490, f32[1536]{0:T(1024)S(1)} %get-tuple-element.488, f32[512]{0:T(512)S(1)} %dynamic_slice.68, f32[32,1536]{1,0:T(8,128)S(1)} %get-tuple-element.489, s32[]{:T(128)S(6)} %select_n.32), kind=kOutput, calls=%fused_computation.15.clone.1 | convolution fusion | flops 306708480 | bytes 1845252 | tf_op jit(solution)/shard_map/while/body/eval_jaxpr/fi,fj->ij/dot_general | solution.py:44
  150.0 0.5 fusion.44
  150.5 0.7 dynamic_slice.66
  153.2 0.7 dynamic_slice.67
  156.1 3.4 %fusion.43 = bf16[512,1536]{1,0:T(8,128)(2,1)S(1)} fusion(f32[32,1536]{1,0:T(8,128)S(1)} %get-tuple-element.490, f32[1536]{0:T(1024)S(1)} %get-tuple-element.488, f32[512]{0:T(512)S(1)} %dynamic_slice.68, f32[32,1536]{1,0:T(8,128)S(1)} %get-tuple-element.489, s32[]{:T(128)S(6)} %select_n.32), kind=kOutput, calls=%fused_computation.15.clone.1 | convolution fusion | flops 306708480 | bytes 1845252 | tf_op jit(solution)/shard_map/while/body/eval_jaxpr/fi,fj->ij/dot_general | solution.py:44
  159.9 0.7 dynamic_slice.66
  162.7 0.7 dynamic_slice.67
  165.5 3.4 %fusion.43 = bf16[512,1536]{1,0:T(8,128)(2,1)S(1)} fusion(f32[32,1536]{1,0:T(8,128)S(1)} %get-tuple-element.490, f32[1536]{0:T(1024)S(1)} %get-tuple-element.488, f32[512]{0:T(512)S(1)} %dynamic_slice.68, f32[32,1536]{1,0:T(8,128)S(1)} %get-tuple-element.489, s32[]{:T(128)S(6)} %select_n.32), kind=kOutput, calls=%fused_computation.15.clone.1 | convolution fusion | flops 306708480 | bytes 1845252 | tf_op jit(solution)/shard_map/while/body/eval_jaxpr/fi,fj->ij/dot_general | solution.py:44
  169.7 11.9 %all_to_all.36 = f32[16,16,96]{2,1,0:T(8,128)S(1)} all-to-all(f32[16,16,96]{2,1,0:T(8,128)S(1)} %copy.21), channel_id=1, replica_groups=mesh['row'=16,'col'=16] {'col'}, dimensions={0} | all-to-all | bytes 196608 | tf_op jit(solution)/shard_map/all_to_all | solution.py:17
  181.6 0.6 broadcast_multiply_fusion
  (59 shorter events, 3.9 us)
Async XLA Ops:
  18.6 18.5 %all-to-all-start.1 = ((f32[16,32,96]{2,1,0:T(8,128)}), f32[16,32,96]{2,1,0:T(8,128)S(1)}, u32[]{:S(2)}, u32[]{:S(2)}) async-start(f32[16,32,96]{2,1,0:T(8,128)} %broadcast_in_dim.39), calls=%async_computation.1 | async-start | bytes 524288 | tf_op jit(solution)/shard_map/all_to_all | solution.py:29
  66.5 11.9 %all-to-all-start.3 = ((f32[16,1,1536]{2,1,0:T(1,128)}), f32[16,1,1536]{2,1,0:T(1,128)S(1)}, u32[]{:S(2)}, u32[]{:S(2)}) async-start(f32[16,1,1536]{2,1,0:T(1,128)} %broadcast_in_dim.41), calls=%async_computation.3 | async-start | bytes 196608 | tf_op jit(solution)/shard_map/all_to_all | solution.py:29
  78.4 36.2 %all-to-all-start.2 = ((f32[16,1,96]{2,1,0:T(1,128)}), f32[16,1,96]{2,1,0:T(1,128)S(1)}, u32[]{:S(2)}, u32[]{:S(2)}) async-start(f32[16,1,96]{2,1,0:T(1,128)} %transpose_reshape_reshape.6), calls=%async_computation.2 | async-start | bytes 16384 | tf_op jit(solution)/shard_map/all_to_all | solution.py:17
  86.0 42.9 %copy-start = (f32[16,96]{1,0:T(8,128)S(1)}, f32[16,96]{1,0:T(8,128)}, u32[]{:S(2)}) copy-start(f32[16,96]{1,0:T(8,128)} %param.9) | copy-start | bytes 18436
  114.6 14.1 %all-to-all-start.4 = ((f32[16,1,96]{2,1,0:T(1,128)}), f32[16,1,96]{2,1,0:T(1,128)S(1)}, u32[]{:S(2)}, u32[]{:S(2)}) async-start(f32[16,1,96]{2,1,0:T(1,128)} %transpose_reshape_reshape.7), calls=%async_computation.4 | async-start | bytes 16384 | tf_op jit(solution)/shard_map/all_to_all | solution.py:17
  129.5 11.4 %all-to-all-start.5 = ((bf16[16,16,96]{2,1,0:T(8,128)(2,1)}), bf16[16,16,96]{2,1,0:T(8,128)(2,1)S(1)}, u32[]{:S(2)}, u32[]{:S(2)}) async-start(bf16[16,16,96]{2,1,0:T(8,128)(2,1)} %broadcast_in_dim.42), calls=%async_computation.5 | async-start | bytes 131072 | tf_op jit(solution)/shard_map/all_to_all | solution.py:29
where the time goes:
time: 183 us; the launch traced here: 182 us
  loops' own time  37.5 us (20%)
  matrix products  33.6 us (18%)
  waiting for transfers between devices  31.9 us (17%)
  starting transfers between devices  30.3 us (17%)
  blocking collectives  29 us (16%)
  local copies, waits for them, and re-layouts  18.7 us (10%)
    dot_general x9, matrix products, kernel_rows(): jnp.einsum('fi,fj->ij', part, col_feat, precision=lax.Precision.HIGHEST)  32.1 us
    all_to_all x3, waiting for transfers between devices, sent_to_all(): return lax.all_to_all(copies, axis, split_axis=0, concat_axis=0, tiled=True)  25 us
    all_to_all x1, blocking collectives, sent_to_all(): return lax.all_to_all(copies, axis, split_axis=0, concat_axis=0, tiled=True)  17.1 us
    all_to_all x3, starting transfers between devices, sent_to_all(): return lax.all_to_all(copies, axis, split_axis=0, concat_axis=0, tiled=True)  15.7 us
    all_to_all x2, starting transfers between devices, sent_and_summed(): lax.all_to_all(parts, axis, split_axis=0, concat_axis=0, tiled=True)  14.6 us
    another operation x1, loops' own time, full_plan(): row_parts, col_parts = lax.map(first_pass, indexes)  12.5 us
    another operation x1, loops' own time, full_plan(): second = combine(lax.map(second_pass, indexes).reshape(1, rows))  12.5 us
    another operation x1, loops' own time, full_plan(): products = lax.map(third_pass, indexes)  12.5 us
  transfers between devices with their start and end apart: 5, of which 4 were waited for; matrix products, arithmetic and copies ran while one was open for 10% of the time, Pallas kernels for 0%

commit v1 on v0

v1 whole, which is shorter than its diff:
```python
import functools
import math

import jax
import jax.numpy as jnp
from jax import lax
from jax.experimental import pallas as pl
from jax.experimental.pallas import tpu as pltpu
from jax.sharding import Mesh, PartitionSpec as P

f32 = jnp.float32
bf16 = jnp.bfloat16
VMEM = pl.BlockSpec(memory_space=pltpu.VMEM)
PARAMS = pltpu.CompilerParams(vmem_limit_bytes=40 * 1024 * 1024)

GROUP_X = "col"
GROUP_Y = "row"


def three_parts(v):
    high = v.astype(bf16)
    rest = v - high.astype(f32)
    mid = rest.astype(bf16)
    low = (rest - mid.astype(f32)).astype(bf16)
    return high, mid, low


def extended(v, left):
    high, mid, low = three_parts(v)
    half = -0.5 * jnp.sum(v * v, axis=0, keepdims=True)
    a, b, c = (p.astype(f32) for p in three_parts(half))
    row = lax.broadcasted_iota(jnp.int32, (16, v.shape[1]), 0)
    base = 0 if left else 3
    ones = jnp.where((row >= 3 - base) & (row < 6 - base), 1.0, 0.0)
    tail = jnp.where(row == base, a, jnp.where(row == base + 1, b, jnp.where(row == base + 2, c, ones)))
    tail = tail.astype(bf16)
    if left:
        parts = [high, high, mid, high, low, mid, tail]
    else:
        parts = [high, mid, high, low, high, mid, tail]
    return jnp.concatenate(parts, axis=0)


def kernel_block(gain, x_ref, y_ref, k_ref, q_ref, col_ref, right_ref):
    count, _, width = x_ref.shape
    total = k_ref.shape[1]
    y = jnp.concatenate([y_ref[i] for i in range(count)], axis=1) * gain
    right_ref[...] = extended(y, False)
    step = 512
    col_ref[...] = jnp.zeros_like(col_ref)
    for i in range(count):
        left = extended(x_ref[i] * gain, True)
        lanes = jnp.zeros((width, 128), f32)
        for j in range(0, total, step):
            expo = lax.dot_general(
                left, right_ref[:, j : j + step], (((0,), (0,)), ((), ())),
                preferred_element_type=f32,
            )
            tile = jnp.exp2(expo).astype(bf16)
            k_ref[i * width : (i + 1) * width, j : j + step] = tile
            wide = tile.astype(f32)
            col_ref[:, j : j + step] += jnp.sum(wide, axis=0, keepdims=True)
            for t in range(0, step, 128):
                lanes = lanes + wide[:, t : t + 128]
        sums = jnp.sum(lanes.T, axis=0, keepdims=True)
        for d in range(count):
            q_ref[d, i : i + 1, :] = sums


def second_block(q_ref, k_ref, col_ref, out_ref):
    count, _, width = q_ref.shape
    total = k_ref.shape[1]
    inv = 1.0 / jnp.sum(q_ref[...], axis=0)
    acc = jnp.zeros((8, total), f32)
    for i in range(count):
        tall = jnp.broadcast_to(inv[i : i + 1, :], (128, width)).T
        for r in range(0, width, 16):
            rows = k_ref[i * width + r : i * width + r + 16, :].astype(f32)
            w = tall[r : r + 16, :]
            prod = jnp.concatenate(
                [rows[:, t : t + 128] * w for t in range(0, total, 128)], axis=1
            )
            acc = acc + prod[:8] + prod[8:]
    second = jnp.sum(acc, axis=0, keepdims=True)
    for d in range(count):
        out_ref[d, 0:1, :] = col_ref[...]
        out_ref[d, 1:2, :] = second


def product_block(m_ref, k_ref, b_ref, out_ref, fac_ref):
    count, _, width = b_ref.shape
    sums = jnp.sum(m_ref[...], axis=0)
    inv = 1.0 / sums[0:1]
    factor = inv * lax.rsqrt(sums[1:2] * inv)
    block = jnp.concatenate([b_ref[i] for i in range(count)], axis=1)
    weighted = (block * factor).astype(bf16)
    for i in range(count):
        out_ref[i] = lax.dot_general(
            weighted, k_ref[i * width : (i + 1) * width, :], (((1,), (1,)), ((), ())),
            preferred_element_type=f32,
        )
        fac_ref[i] = factor[:, i * width : (i + 1) * width]


def per_device(features, block):
    width, owned = features.shape
    n = lax.axis_size(GROUP_X)
    m = lax.axis_size(GROUP_Y)
    frames = owned * n * m
    scale = 4.0 / (float(frames) ** (2.0 / width) - 1.0)
    gain = math.sqrt(2.0 * math.log2(math.e) / scale)
    k_rows, k_cols = n * owned, m * owned

    def to_all(x, axis):
        copies = jnp.broadcast_to(x, (lax.axis_size(axis), *x.shape))
        return lax.all_to_all(copies, axis, 0, 0, tiled=True)

    x_feat = lax.all_gather(features, GROUP_X)
    y_block = lax.all_gather(block, GROUP_Y)
    y_feat = to_all(features, GROUP_Y)
    kern, q_parts, col_sum = pl.pallas_call(
        functools.partial(kernel_block, gain),
        out_shape=(
            jax.ShapeDtypeStruct((k_rows, k_cols), bf16),
            jax.ShapeDtypeStruct((n, n, owned), f32),
            jax.ShapeDtypeStruct((1, k_cols), f32),
        ),
        in_specs=[VMEM] * 2,
        out_specs=(VMEM,) * 3,
        scratch_shapes=[pltpu.VMEM((6 * width + 16, k_cols), bf16)],
        compiler_params=PARAMS,
        name="kernel_block",
    )(x_feat, y_feat)
    q_parts = lax.all_to_all(q_parts, GROUP_X, 0, 0, tiled=True)
    sums = pl.pallas_call(
        second_block,
        out_shape=jax.ShapeDtypeStruct((m, 2, k_cols), f32),
        in_specs=[VMEM] * 3,
        out_specs=VMEM,
        compiler_params=PARAMS,
        name="second_block",
    )(q_parts, kern, col_sum)
    sums = lax.all_to_all(sums, GROUP_Y, 0, 0, tiled=True)
    parts, factor = pl.pallas_call(
        product_block,
        out_shape=(
            jax.ShapeDtypeStruct((n, block.shape[0], owned), f32),
            jax.ShapeDtypeStruct((m, 1, owned), f32),
        ),
        in_specs=[VMEM] * 3,
        out_specs=(VMEM,) * 2,
        compiler_params=PARAMS,
        name="product_block",
    )(sums, kern, y_block)
    parts = lax.all_to_all(parts, GROUP_X, 0, 0, tiled=True)
    own = lax.dynamic_index_in_dim(factor, lax.axis_index(GROUP_Y), 0, keepdims=False)
    return jnp.sum(parts, axis=0) * own


def solution(mesh):
    placed = (P(None, ("row", "col")), P(None, ("row", "col")))
    return jax.shard_map(
        per_device, mesh=mesh, in_specs=placed, out_specs=P(None, ("row", "col")), check_vma=False
    )
```

time: 183 us -> 113 us (0.62)
  loops' own time: 37.5 us -> 0 us
  blocking collectives: 29 us -> 63.5 us
  matrix products: 33.6 us -> 0 us
  waiting for transfers between devices: 31.9 us -> 7.65 us
  local copies, waits for them, and re-layouts: 18.7 us -> 5.93 us
  Pallas kernels: 0 us -> 6.23 us
  starting transfers between devices: 30.3 us -> 28.1 us
    all_gather x0 -> x2, blocking collectives: none -> 53.3 us  [the longest x1 27.4 us: per_device(): y_block = lax.all_gather(block, GROUP_Y)]
    another operation x3 -> x0, loops' own time: 37.5 us -> none  [the longest x1 12.5 us: full_plan(): row_parts, col_parts = lax.map(first_pass, indexes)]
    dot_general x12 -> x0, matrix products: 33.6 us -> none  [the longest x9 32.1 us: kernel_rows(): jnp.einsum('fi,fj->ij', part, col_feat, precision=lax.Precision.HIGHEST)]
    all_to_all x5 -> x3, waiting for transfers between devices: 31.9 us -> 7.65 us  [the longest x1 7.65 us: per_device(): parts = lax.all_to_all(parts, GROUP_X, 0, 0, tiled=True)]
    all_to_all x2 -> x1, blocking collectives: 29 us -> 10.2 us  [per_device(): q_parts = lax.all_to_all(q_parts, GROUP_X, 0, 0, tiled=True)]
    dynamic_slice x27 -> x0, local copies, waits for them, and re-layouts: 12.8 us -> none  [the longest x9 6.03 us: full_plan(): row_parts, col_parts = lax.map(first_pass, indexes)]
    pallas_call x0 -> x3, Pallas kernels: none -> 6.23 us  [the longest x1 2.44 us: per_device(): pl.pallas_call(functools.partial(kernel_block, gain), out_shape=(jax.Shap...]
    unnamed x2 -> x6, local copies, waits for them, and re-layouts: 0.01 us -> 4.48 us
  transfers between devices with their start and end apart: 5 -> 3, of which waited for: 4 -> 1; matrix products, arithmetic and copies ran while one was open for 10% -> 0% of each run, Pallas kernels for 0% -> 0%
where the time goes in v1:
time: 113 us; the launch traced here: 112 us
  blocking collectives  63.5 us (56%)
  starting transfers between devices  28.1 us (25%)
  waiting for transfers between devices  7.65 us (7%)
  Pallas kernels  6.23 us (6%)
  local copies, waits for them, and re-layouts  5.93 us (5%)
    all_gather x1, blocking collectives, per_device(): y_block = lax.all_gather(block, GROUP_Y)  27.4 us
    all_gather x1, blocking collectives, per_device(): x_feat = lax.all_gather(features, GROUP_X)  25.9 us
    all_to_all x1, starting transfers between devices, per_device(): parts = lax.all_to_all(parts, GROUP_X, 0, 0, tiled=True)  10.9 us
    all_to_all x1, blocking collectives, per_device(): q_parts = lax.all_to_all(q_parts, GROUP_X, 0, 0, tiled=True)  10.2 us
    all_to_all x1, starting transfers between devices, to_all(): return lax.all_to_all(copies, axis, 0, 0, tiled=True)  10.1 us
    all_to_all x1, waiting for transfers between devices, per_device(): parts = lax.all_to_all(parts, GROUP_X, 0, 0, tiled=True)  7.65 us
    all_to_all x1, starting transfers between devices, per_device(): sums = lax.all_to_all(sums, GROUP_Y, 0, 0, tiled=True)  7.09 us
    unnamed x6, local copies, waits for them, and re-layouts  4.48 us
  transfers between devices with their start and end apart: 3, of which 1 were waited for; matrix products, arithmetic and copies ran while one was open for 0% of the time, Pallas kernels for 0%

profile of v1, /device:TPU:1, one launch (start us, length us, event | category | flops | bytes accessed | tf_op | source)
XLA Modules:
  0.0 112.1 jit_solution(16035545082201193774)
XLA Ops:
  0.0 0.0 copy-start.2
  0.0 1.4 %broadcast_in_dim.3 = f32[16,32,96]{2,1,0:T(8,128)} broadcast(f32[32,96]{1,0:T(8,128)} %param.2), dimensions={1,2} | broadcast | bytes 208896 | tf_op jit(solution)/shard_map/broadcast_in_dim | solution.py:115
  1.5 10.1 %all-to-all-start = ((f32[16,32,96]{2,1,0:T(8,128)}), f32[16,32,96]{2,1,0:T(8,128)S(1)}, u32[]{:S(2)}, u32[]{:S(2)}) async-start(f32[16,32,96]{2,1,0:T(8,128)} %broadcast_in_dim.3), calls=%async_computation | async-start | bytes 524288 | tf_op jit(solution)/shard_map/all_to_all | solution.py:116
  11.6 25.9 %all-gather = f32[512,96]{1,0:T(8,128)S(1)} all-gather(f32[32,96]{1,0:T(8,128)} %param.2), channel_id=2, replica_groups=mesh['row'=16,'col'=16] {'col'}, dimensions={0}, use_global_device_ids=true | all-gather | bytes 208896 | tf_op jit(solution)/shard_map/all_gather | solution.py:118
  37.5 0.0 all-to-all-done.y_ref
  37.5 2.4 %kernel_block.1 = (bf16[1536,1536]{1,0:T(8,128)(2,1)S(1)}, f32[16,16,96]{2,1,0:T(8,128)S(1)}, f32[1,1536]{1,0:T(1,128)S(1)}) custom-call(f32[16,32,96]{2,1,0:T(8,128)S(1)} %bitcast.4, f32[16,32,96]{2,1,0:T(8,128)S(1)} %all-to-all-done.y_ref), custom_call_target="tpu_custom_call" | custom-call | tf_op jit(solution)/shard_map/kernel_block/pallas_call | solution.py:121
  39.9 10.2 %all_to_all.20.q_ref = f32[16,16,96]{2,1,0:T(8,128)S(1)} all-to-all(f32[16,16,96]{2,1,0:T(8,128)S(1)} %get-tuple-element.10), channel_id=1, replica_groups=mesh['row'=16,'col'=16] {'col'}, dimensions={0} | all-to-all | bytes 196608 | tf_op jit(solution)/shard_map/all_to_all | solution.py:134
  50.2 1.8 %second_block.1 = f32[16,2,1536]{2,1,0:T(2,128)} custom-call(f32[16,16,96]{2,1,0:T(8,128)S(1)} %all_to_all.20.q_ref, bf16[1536,1536]{1,0:T(8,128)(2,1)S(1)} %get-tuple-element.11.k_ref, f32[1,1536]{1,0:T(1,128)S(1)} %get-tuple-element.12.col_ref), custom_call_target="tpu_custom_call" | custom-call | tf_op jit(solution)/shard_map/second_block/pallas_call | solution.py:135
  51.9 0.0 copy-start
  51.9 2.1 %copy-done = bf16[1536,1536]{1,0:T(8,128)(2,1)} copy-done((bf16[1536,1536]{1,0:T(8,128)(2,1)}, bf16[1536,1536]{1,0:T(8,128)(2,1)S(1)}, u32[]{:S(2)}) %copy-start) | copy-done | bytes 4718616
  54.1 7.1 %all-to-all-start.2 = ((f32[16,2,1536]{2,1,0:T(2,128)}), f32[16,2,1536]{2,1,0:T(2,128)S(1)}, u32[]{:S(2)}, u32[]{:S(2)}) async-start(f32[16,2,1536]{2,1,0:T(2,128)} %second_block.1), calls=%async_computation.2 | async-start | bytes 393216 | tf_op jit(solution)/shard_map/all_to_all | solution.py:143
  61.2 0.0 copy-done.2
  61.2 27.4 %all-gather.1 = f32[256,96]{1,0:T(8,128)S(1)} all-gather(f32[16,96]{1,0:T(8,128)S(1)} %copy-done.2), channel_id=3, replica_groups=mesh['row'=16,'col'=16] {'row'}, dimensions={0}, use_global_device_ids=true | all-gather | bytes 104448 | tf_op jit(solution)/shard_map/all_gather | solution.py:119
  88.6 0.0 all-to-all-done.2.m_ref
  88.6 0.0 copy-start.1
  88.6 2.3 %copy-done.1 = bf16[1536,1536]{1,0:T(8,128)(2,1)S(1)} copy-done((bf16[1536,1536]{1,0:T(8,128)(2,1)S(1)}, bf16[1536,1536]{1,0:T(8,128)(2,1)}, u32[]{:S(2)}) %copy-start.1) | copy-done | bytes 4718616
  90.9 2.0 %product_block.1 = (f32[16,16,96]{2,1,0:T(8,128)}, f32[16,1,96]{2,1,0:T(1,128)S(1)}) custom-call(f32[16,2,1536]{2,1,0:T(2,128)S(1)} %all-to-all-done.2.m_ref, bf16[1536,1536]{1,0:T(8,128)(2,1)S(1)} %copy-done.1, f32[16,16,96]{2,1,0:T(8,128)S(1)} %bitcast.5), custom_call_target="tpu_custom_call" | custom-call | tf_op jit(solution)/shard_map/product_block/pallas_call | solution.py:144
  92.9 10.9 %all-to-all-start.3 = ((f32[16,16,96]{2,1,0:T(8,128)}), f32[16,16,96]{2,1,0:T(8,128)S(1)}, u32[]{:S(2)}, u32[]{:S(2)}) async-start(f32[16,16,96]{2,1,0:T(8,128)} %get-tuple-element.13), calls=%async_computation.3 | async-start | bytes 262144 | tf_op jit(solution)/shard_map/all_to_all | solution.py:155
  103.8 7.6 %all-to-all-done.3 = f32[16,16,96]{2,1,0:T(8,128)S(1)} async-done(((f32[16,16,96]{2,1,0:T(8,128)}), f32[16,16,96]{2,1,0:T(8,128)S(1)}, u32[]{:S(2)}, u32[]{:S(2)}) %all-to-all-start.3) | async-done | bytes 98336 | tf_op jit(solution)/shard_map/all_to_all | solution.py:155
  111.5 0.6 broadcast_multiply_fusion
  (2 shorter events, 0.0 us)
Async XLA Ops:
  0.0 61.2 %copy-start.2 = (f32[16,96]{1,0:T(8,128)S(1)}, f32[16,96]{1,0:T(8,128)}, u32[]{:S(2)}) copy-start(f32[16,96]{1,0:T(8,128)} %param.3) | copy-start | bytes 18436
  1.5 36.0 %all-to-all-start = ((f32[16,32,96]{2,1,0:T(8,128)}), f32[16,32,96]{2,1,0:T(8,128)S(1)}, u32[]{:S(2)}, u32[]{:S(2)}) async-start(f32[16,32,96]{2,1,0:T(8,128)} %broadcast_in_dim.3), calls=%async_computation | async-start | bytes 524288 | tf_op jit(solution)/shard_map/all_to_all | solution.py:116
  51.9 2.1 %copy-start = (bf16[1536,1536]{1,0:T(8,128)(2,1)}, bf16[1536,1536]{1,0:T(8,128)(2,1)S(1)}, u32[]{:S(2)}) copy-start(bf16[1536,1536]{1,0:T(8,128)(2,1)S(1)} %get-tuple-element.11.k_ref) | copy-start | bytes 14155780
  54.1 34.5 %all-to-all-start.2 = ((f32[16,2,1536]{2,1,0:T(2,128)}), f32[16,2,1536]{2,1,0:T(2,128)S(1)}, u32[]{:S(2)}, u32[]{:S(2)}) async-start(f32[16,2,1536]{2,1,0:T(2,128)} %second_block.1), calls=%async_computation.2 | async-start | bytes 393216 | tf_op jit(solution)/shard_map/all_to_all | solution.py:143
  88.6 2.3 %copy-start.1 = (bf16[1536,1536]{1,0:T(8,128)(2,1)S(1)}, bf16[1536,1536]{1,0:T(8,128)(2,1)}, u32[]{:S(2)}) copy-start(bf16[1536,1536]{1,0:T(8,128)(2,1)} %copy-done) | copy-start | bytes 14155780
  92.9 18.6 %all-to-all-start.3 = ((f32[16,16,96]{2,1,0:T(8,128)}), f32[16,16,96]{2,1,0:T(8,128)S(1)}, u32[]{:S(2)}, u32[]{:S(2)}) async-start(f32[16,16,96]{2,1,0:T(8,128)} %get-tuple-element.13), calls=%async_computation.3 | async-start | bytes 262144 | tf_op jit(solution)/shard_map/all_to_all | solution.py:155

commit v2 on v1

--- a/solution.py
+++ b/solution.py
@@ -11,10 +11,11 @@
 f32 = jnp.float32
 bf16 = jnp.bfloat16
 VMEM = pl.BlockSpec(memory_space=pltpu.VMEM)
-PARAMS = pltpu.CompilerParams(vmem_limit_bytes=40 * 1024 * 1024)
+PARAMS = pltpu.CompilerParams(vmem_limit_bytes=16 * 1024 * 1024)
 
-GROUP_X = "col"
-GROUP_Y = "row"
+ALL = ("z", "ylo", "yhi", "x", "core")
+GROUP_X = ("ylo", "yhi", "x")
+GROUP_Y = ("z", "core")
 
 
 def three_parts(v):
@@ -41,10 +42,19 @@
     return jnp.concatenate(parts, axis=0)
 
 
+def spread_block(f_ref, b_ref, x_ref, y_ref):
+    width = f_ref.shape[0]
+    values = f_ref[...]
+    for i in range(x_ref.shape[0]):
+        x_ref[i] = values
+    y_ref[:width] = values
+    y_ref[width:] = b_ref[...]
+
+
 def kernel_block(gain, x_ref, y_ref, k_ref, q_ref, col_ref, right_ref):
-    count, _, width = x_ref.shape
+    count, size, width = x_ref.shape
     total = k_ref.shape[1]
-    y = jnp.concatenate([y_ref[i] for i in range(count)], axis=1) * gain
+    y = jnp.concatenate([y_ref[i, :size] for i in range(count)], axis=1) * gain
     right_ref[...] = extended(y, False)
     step = 512
     col_ref[...] = jnp.zeros_like(col_ref)
@@ -88,11 +98,12 @@
 
 
 def product_block(m_ref, k_ref, b_ref, out_ref, fac_ref):
-    count, _, width = b_ref.shape
+    count, rows, width = b_ref.shape
+    size = rows - out_ref.shape[1]
     sums = jnp.sum(m_ref[...], axis=0)
     inv = 1.0 / sums[0:1]
     factor = inv * lax.rsqrt(sums[1:2] * inv)
-    block = jnp.concatenate([b_ref[i] for i in range(count)], axis=1)
+    block = jnp.concatenate([b_ref[i, size:] for i in range(count)], axis=1)
     weighted = (block * factor).astype(bf16)
     for i in range(count):
         out_ref[i] = lax.dot_general(
@@ -111,13 +122,19 @@
     gain = math.sqrt(2.0 * math.log2(math.e) / scale)
     k_rows, k_cols = n * owned, m * owned
 
-    def to_all(x, axis):
-        copies = jnp.broadcast_to(x, (lax.axis_size(axis), *x.shape))
-        return lax.all_to_all(copies, axis, 0, 0, tiled=True)
-
-    x_feat = lax.all_gather(features, GROUP_X)
-    y_block = lax.all_gather(block, GROUP_Y)
-    y_feat = to_all(features, GROUP_Y)
+    copies, both = pl.pallas_call(
+        spread_block,
+        out_shape=(
+            jax.ShapeDtypeStruct((n, width, owned), f32),
+            jax.ShapeDtypeStruct((width + block.shape[0], owned), f32),
+        ),
+        in_specs=[VMEM] * 2,
+        out_specs=(VMEM,) * 2,
+        compiler_params=PARAMS,
+        name="spread_block",
+    )(features, block)
+    x_feat = lax.all_to_all(copies, GROUP_X, 0, 0, tiled=True)
+    y_both = lax.all_gather(both, GROUP_Y)
     kern, q_parts, col_sum = pl.pallas_call(
         functools.partial(kernel_block, gain),
         out_shape=(
@@ -130,7 +147,7 @@
         scratch_shapes=[pltpu.VMEM((6 * width + 16, k_cols), bf16)],
         compiler_params=PARAMS,
         name="kernel_block",
-    )(x_feat, y_feat)
+    )(x_feat, y_both)
     q_parts = lax.all_to_all(q_parts, GROUP_X, 0, 0, tiled=True)
     sums = pl.pallas_call(
         second_block,
@@ -151,14 +168,15 @@
         out_specs=(VMEM,) * 2,
         compiler_params=PARAMS,
         name="product_block",
-    )(sums, kern, y_block)
+    )(sums, kern, y_both)
     parts = lax.all_to_all(parts, GROUP_X, 0, 0, tiled=True)
     own = lax.dynamic_index_in_dim(factor, lax.axis_index(GROUP_Y), 0, keepdims=False)
     return jnp.sum(parts, axis=0) * own
 
 
 def solution(mesh):
-    placed = (P(None, ("row", "col")), P(None, ("row", "col")))
+    fine = Mesh(mesh.devices.reshape(mesh.shape["row"] // 2, 2, 2, mesh.shape["col"] // 4, 2), ALL)
+    placed = P(None, ALL)
     return jax.shard_map(
-        per_device, mesh=mesh, in_specs=placed, out_specs=P(None, ("row", "col")), check_vma=False
+        per_device, mesh=fine, in_specs=(placed, placed), out_specs=placed, check_vma=False
     )

time: 113 us -> 83.7 us (0.74)
  blocking collectives: 63.5 us -> 35.4 us
  starting transfers between devices: 28.1 us -> 16.3 us
  waiting for transfers between devices: 7.65 us -> 17.8 us
    all_gather x2 -> x1, blocking collectives: 53.3 us -> 21.8 us  [per_device(): y_both = lax.all_gather(both, GROUP_Y)]
    all_to_all x1, waiting for transfers between devices: 0.01 us -> 10.3 us  [per_device(): sums = lax.all_to_all(sums, GROUP_Y, 0, 0, tiled=True)]
    all_to_all x1, starting transfers between devices: 10.9 us -> 3.51 us  [per_device(): parts = lax.all_to_all(parts, GROUP_X, 0, 0, tiled=True)]
    all_to_all x1, blocking collectives: 10.2 us -> 13.6 us  [per_device(): q_parts = lax.all_to_all(q_parts, GROUP_X, 0, 0, tiled=True)]
    all_to_all x1, starting transfers between devices: 10.1 us -> 7.58 us  [per_device(): x_feat = lax.all_to_all(copies, GROUP_X, 0, 0, tiled=True)]
    all_to_all x1, starting transfers between devices: 7.09 us -> 5.23 us  [per_device(): sums = lax.all_to_all(sums, GROUP_Y, 0, 0, tiled=True)]
    broadcast_in_dim x1 -> x0, local copies, waits for them, and re-layouts: 1.45 us -> none  [to_all(): copies = jnp.broadcast_to(x, (lax.axis_size(axis), *x.shape))]
    unnamed x6 -> x8, local copies, waits for them, and re-layouts: 4.48 us -> 5.89 us
  transfers between devices with their start and end apart: 3 -> 3, of which waited for: 1 -> 2; matrix products, arithmetic and copies ran while one was open for 0% -> 0% of each run, Pallas kernels for 0% -> 0%
where the time goes in v2:
time: 83.7 us; the launch traced here: 83.1 us
  blocking collectives  35.4 us (42%)
  waiting for transfers between devices  17.8 us (21%)
  starting transfers between devices  16.3 us (19%)
  Pallas kernels  6.96 us (8%)
  local copies, waits for them, and re-layouts  5.9 us (7%)
    all_gather x1, blocking collectives, per_device(): y_both = lax.all_gather(both, GROUP_Y)  21.8 us
    all_to_all x1, blocking collectives, per_device(): q_parts = lax.all_to_all(q_parts, GROUP_X, 0, 0, tiled=True)  13.6 us
    all_to_all x1, waiting for transfers between devices, per_device(): sums = lax.all_to_all(sums, GROUP_Y, 0, 0, tiled=True)  10.3 us
    all_to_all x1, starting transfers between devices, per_device(): x_feat = lax.all_to_all(copies, GROUP_X, 0, 0, tiled=True)  7.58 us
    all_to_all x1, waiting for transfers between devices, per_device(): parts = lax.all_to_all(parts, GROUP_X, 0, 0, tiled=True)  7.47 us
    unnamed x8, local copies, waits for them, and re-layouts  5.89 us
    all_to_all x1, starting transfers between devices, per_device(): sums = lax.all_to_all(sums, GROUP_Y, 0, 0, tiled=True)  5.23 us
    all_to_all x1, starting transfers between devices, per_device(): parts = lax.all_to_all(parts, GROUP_X, 0, 0, tiled=True)  3.51 us
  transfers between devices with their start and end apart: 3, of which 2 were waited for; matrix products, arithmetic and copies ran while one was open for 0% of the time, Pallas kernels for 0%

profile of v2, /device:TPU:1, one launch (start us, length us, event | category | flops | bytes accessed | tf_op | source)
XLA Modules:
  0.0 83.1 jit_solution(14270840835948234628)
XLA Ops:
  0.0 0.0 copy-start.2
  0.0 0.7 copy-done.2
  0.7 0.0 copy-start.3
  0.7 0.7 copy-done.3
  1.4 0.7 spread_block.1
  2.2 7.6 %all-to-all-start = ((f32[16,32,96]{2,1,0:T(8,128)}), f32[16,32,96]{2,1,0:T(8,128)S(1)}, u32[]{:S(2)}, u32[]{:S(2)}) async-start(f32[16,32,96]{2,1,0:T(8,128)} %get-tuple-element.12), calls=%async_computation | async-start | bytes 524288 | tf_op jit(solution)/shard_map/all_to_all | solution.py:136
  9.7 21.8 %all-gather = f32[768,96]{1,0:T(8,128)S(1)} all-gather(f32[48,96]{1,0:T(8,128)S(1)} %get-tuple-element.13), channel_id=2, replica_groups=mesh['z'=8,'ylo'=2,'yhi'=2,'x'=4,'core'=2] {'z','core'}, dimensions={0}, use_global_device_ids=true | all-gather | bytes 313344 | tf_op jit(solution)/shard_map/all_gather | solution.py:137
  31.6 0.0 all-to-all-done.x_ref
  31.6 2.4 %kernel_block.1 = (bf16[1536,1536]{1,0:T(8,128)(2,1)S(1)}, f32[16,16,96]{2,1,0:T(8,128)S(1)}, f32[1,1536]{1,0:T(1,128)S(1)}) custom-call(f32[16,32,96]{2,1,0:T(8,128)S(1)} %all-to-all-done.x_ref, f32[16,48,96]{2,1,0:T(8,128)S(1)} %bitcast.3), custom_call_target="tpu_custom_call" | custom-call | tf_op jit(solution)/shard_map/kernel_block/pallas_call | solution.py:138
  34.0 13.6 %all_to_all.20.q_ref = f32[16,16,96]{2,1,0:T(8,128)S(1)} all-to-all(f32[16,16,96]{2,1,0:T(8,128)S(1)} %get-tuple-element.14), channel_id=1, replica_groups=mesh['z'=8,'ylo'=2,'yhi'=2,'x'=4,'core'=2] {'ylo','yhi','x'}, dimensions={0} | all-to-all | bytes 196608 | tf_op jit(solution)/shard_map/all_to_all | solution.py:151
  47.6 1.8 %second_block.1 = f32[16,2,1536]{2,1,0:T(2,128)} custom-call(f32[16,16,96]{2,1,0:T(8,128)S(1)} %all_to_all.20.q_ref, bf16[1536,1536]{1,0:T(8,128)(2,1)S(1)} %get-tuple-element.15.k_ref, f32[1,1536]{1,0:T(1,128)S(1)} %get-tuple-element.16.col_ref), custom_call_target="tpu_custom_call" | custom-call | tf_op jit(solution)/shard_map/second_block/pallas_call | solution.py:152
  49.4 0.0 copy-start
  49.4 2.1 %copy-done = bf16[1536,1536]{1,0:T(8,128)(2,1)} copy-done((bf16[1536,1536]{1,0:T(8,128)(2,1)}, bf16[1536,1536]{1,0:T(8,128)(2,1)S(1)}, u32[]{:S(2)}) %copy-start) | copy-done | bytes 4718616
  51.5 5.2 %all-to-all-start.2 = ((f32[16,2,1536]{2,1,0:T(2,128)}), f32[16,2,1536]{2,1,0:T(2,128)S(1)}, u32[]{:S(2)}, u32[]{:S(2)}) async-start(f32[16,2,1536]{2,1,0:T(2,128)} %second_block.1), calls=%async_computation.2 | async-start | bytes 393216 | tf_op jit(solution)/shard_map/all_to_all | solution.py:160
  56.7 10.3 %all-to-all-done.2.m_ref = f32[16,2,1536]{2,1,0:T(2,128)S(1)} async-done(((f32[16,2,1536]{2,1,0:T(2,128)}), f32[16,2,1536]{2,1,0:T(2,128)S(1)}, u32[]{:S(2)}, u32[]{:S(2)}) %all-to-all-start.2) | async-done | bytes 196640 | tf_op jit(solution)/shard_map/all_to_all | solution.py:160
  67.1 0.0 copy-start.1
  67.1 2.3 %copy-done.1 = bf16[1536,1536]{1,0:T(8,128)(2,1)S(1)} copy-done((bf16[1536,1536]{1,0:T(8,128)(2,1)S(1)}, bf16[1536,1536]{1,0:T(8,128)(2,1)}, u32[]{:S(2)}) %copy-start.1) | copy-done | bytes 4718616
  69.4 2.0 %product_block.1 = (f32[16,16,96]{2,1,0:T(8,128)}, f32[16,1,96]{2,1,0:T(1,128)S(1)}) custom-call(f32[16,2,1536]{2,1,0:T(2,128)S(1)} %all-to-all-done.2.m_ref, bf16[1536,1536]{1,0:T(8,128)(2,1)S(1)} %copy-done.1, f32[16,48,96]{2,1,0:T(8,128)S(1)} %bitcast.4), custom_call_target="tpu_custom_call" | custom-call | tf_op jit(solution)/shard_map/product_block/pallas_call | solution.py:161
  71.4 3.5 %all-to-all-start.3 = ((f32[16,16,96]{2,1,0:T(8,128)}), f32[16,16,96]{2,1,0:T(8,128)S(1)}, u32[]{:S(2)}, u32[]{:S(2)}) async-start(f32[16,16,96]{2,1,0:T(8,128)} %get-tuple-element.17), calls=%async_computation.3 | async-start | bytes 262144 | tf_op jit(solution)/shard_map/all_to_all | solution.py:172
  75.0 7.5 %all-to-all-done.3 = f32[16,16,96]{2,1,0:T(8,128)S(1)} async-done(((f32[16,16,96]{2,1,0:T(8,128)}), f32[16,16,96]{2,1,0:T(8,128)S(1)}, u32[]{:S(2)}, u32[]{:S(2)}) %all-to-all-start.3) | async-done | bytes 98336 | tf_op jit(solution)/shard_map/all_to_all | solution.py:172
  82.5 0.6 broadcast_multiply_fusion
  (2 shorter events, 0.0 us)
Async XLA Ops:
  0.0 0.7 copy-start.2
  0.7 0.7 copy-start.3
  2.2 29.4 %all-to-all-start = ((f32[16,32,96]{2,1,0:T(8,128)}), f32[16,32,96]{2,1,0:T(8,128)S(1)}, u32[]{:S(2)}, u32[]{:S(2)}) async-start(f32[16,32,96]{2,1,0:T(8,128)} %get-tuple-element.12), calls=%async_computation | async-start | bytes 524288 | tf_op jit(solution)/shard_map/all_to_all | solution.py:136
  49.4 2.1 %copy-start = (bf16[1536,1536]{1,0:T(8,128)(2,1)}, bf16[1536,1536]{1,0:T(8,128)(2,1)S(1)}, u32[]{:S(2)}) copy-start(bf16[1536,1536]{1,0:T(8,128)(2,1)S(1)} %get-tuple-element.15.k_ref) | copy-start | bytes 14155780
  51.5 15.6 %all-to-all-start.2 = ((f32[16,2,1536]{2,1,0:T(2,128)}), f32[16,2,1536]{2,1,0:T(2,128)S(1)}, u32[]{:S(2)}, u32[]{:S(2)}) async-start(f32[16,2,1536]{2,1,0:T(2,128)} %second_block.1), calls=%async_computation.2 | async-start | bytes 393216 | tf_op jit(solution)/shard_map/all_to_all | solution.py:160
  67.1 2.3 %copy-start.1 = (bf16[1536,1536]{1,0:T(8,128)(2,1)S(1)}, bf16[1536,1536]{1,0:T(8,128)(2,1)}, u32[]{:S(2)}) copy-start(bf16[1536,1536]{1,0:T(8,128)(2,1)} %copy-done) | copy-start | bytes 14155780
  71.4 11.0 %all-to-all-start.3 = ((f32[16,16,96]{2,1,0:T(8,128)}), f32[16,16,96]{2,1,0:T(8,128)S(1)}, u32[]{:S(2)}, u32[]{:S(2)}) async-start(f32[16,16,96]{2,1,0:T(8,128)} %get-tuple-element.17), calls=%async_computation.3 | async-start | bytes 262144 | tf_op jit(solution)/shard_map/all_to_all | solution.py:172

commit v3 on v2

--- a/solution.py
+++ b/solution.py
@@ -14,8 +14,15 @@
 PARAMS = pltpu.CompilerParams(vmem_limit_bytes=16 * 1024 * 1024)
 
 ALL = ("z", "ylo", "yhi", "x", "core")
-GROUP_X = ("ylo", "yhi", "x")
-GROUP_Y = ("z", "core")
+GROUP_X = ("ylo", "x", "core")
+GROUP_Y = ("z", "yhi")
+
+
+def place_in(axes):
+    place = 0
+    for name in axes:
+        place = place * lax.axis_size(name) + lax.axis_index(name)
+    return place
 
 
 def three_parts(v):
@@ -42,24 +49,33 @@
     return jnp.concatenate(parts, axis=0)
 
 
-def spread_block(f_ref, b_ref, x_ref, y_ref):
+def spread_block(f_ref, b_ref, y_ref, f_here, b_here, sems):
     width = f_ref.shape[0]
-    values = f_ref[...]
-    for i in range(x_ref.shape[0]):
-        x_ref[i] = values
-    y_ref[:width] = values
-    y_ref[width:] = b_ref[...]
-
-
-def kernel_block(gain, x_ref, y_ref, k_ref, q_ref, col_ref, right_ref):
-    count, size, width = x_ref.shape
+    first = pltpu.make_async_copy(f_ref, f_here, sems.at[0])
+    second = pltpu.make_async_copy(b_ref, b_here, sems.at[1])
+    first.start()
+    second.start()
+    first.wait()
+    second.wait()
+    values = jnp.concatenate([f_here[...], b_here[...]], axis=0)
+    for i in range(y_ref.shape[0]):
+        y_ref[i] = values
+
+
+def kernel_block(gain, near_ref, far_ref, y_ref, k_ref, q_ref, col_ref, right_ref):
+    half, size, width = near_ref.shape
+    count = 2 * half
+    me = place_in(GROUP_X)
     total = k_ref.shape[1]
     y = jnp.concatenate([y_ref[i, :size] for i in range(count)], axis=1) * gain
     right_ref[...] = extended(y, False)
     step = 512
     col_ref[...] = jnp.zeros_like(col_ref)
-    for i in range(count):
-        left = extended(x_ref[i] * gain, True)
+    for s in range(count):
+        frames = near_ref[s] if s < half else far_ref[s - half]
+        left = extended(frames * gain, True)
+        i = jnp.bitwise_xor(me, s)
+        rows = pl.ds(pl.multiple_of(i * width, 32), width)
         lanes = jnp.zeros((width, 128), f32)
         for j in range(0, total, step):
             expo = lax.dot_general(
@@ -67,14 +83,14 @@
                 preferred_element_type=f32,
             )
             tile = jnp.exp2(expo).astype(bf16)
-            k_ref[i * width : (i + 1) * width, j : j + step] = tile
+            k_ref[rows, j : j + step] = tile
             wide = tile.astype(f32)
             col_ref[:, j : j + step] += jnp.sum(wide, axis=0, keepdims=True)
             for t in range(0, step, 128):
                 lanes = lanes + wide[:, t : t + 128]
         sums = jnp.sum(lanes.T, axis=0, keepdims=True)
         for d in range(count):
-            q_ref[d, i : i + 1, :] = sums
+            q_ref[d, pl.ds(i, 1), :] = sums
 
 
 def second_block(q_ref, k_ref, col_ref, out_ref):
@@ -97,7 +113,7 @@
         out_ref[d, 1:2, :] = second
 
 
-def product_block(m_ref, k_ref, b_ref, out_ref, fac_ref):
+def product_block(m_ref, k_ref, b_ref, out_ref, own_ref, fac_ref):
     count, rows, width = b_ref.shape
     size = rows - out_ref.shape[1]
     sums = jnp.sum(m_ref[...], axis=0)
@@ -111,6 +127,7 @@
             preferred_element_type=f32,
         )
         fac_ref[i] = factor[:, i * width : (i + 1) * width]
+    own_ref[...] = fac_ref[place_in(GROUP_Y)]
 
 
 def per_device(features, block):
@@ -122,19 +139,27 @@
     gain = math.sqrt(2.0 * math.log2(math.e) / scale)
     k_rows, k_cols = n * owned, m * owned
 
-    copies, both = pl.pallas_call(
+    held = features[None]
+    received = held
+    for axis, step in (("core", 1), ("x", 1), ("x", 2), ("ylo", 1)):
+        pairs = [(k, k ^ step) for k in range(lax.axis_size(axis))]
+        if received is not held:
+            held = jnp.concatenate([held, received], axis=0)
+        received = lax.ppermute(held, axis, pairs)
+    copies = pl.pallas_call(
         spread_block,
-        out_shape=(
-            jax.ShapeDtypeStruct((n, width, owned), f32),
-            jax.ShapeDtypeStruct((width + block.shape[0], owned), f32),
-        ),
-        in_specs=[VMEM] * 2,
-        out_specs=(VMEM,) * 2,
+        out_shape=jax.ShapeDtypeStruct((m, width + block.shape[0], owned), f32),
+        in_specs=[pl.BlockSpec(memory_space=pltpu.HBM)] * 2,
+        out_specs=VMEM,
+        scratch_shapes=[
+            pltpu.VMEM((width, owned), f32),
+            pltpu.VMEM(block.shape, f32),
+            pltpu.SemaphoreType.DMA((2,)),
+        ],
         compiler_params=PARAMS,
         name="spread_block",
     )(features, block)
-    x_feat = lax.all_to_all(copies, GROUP_X, 0, 0, tiled=True)
-    y_both = lax.all_gather(both, GROUP_Y)
+    y_both = lax.all_to_all(copies, GROUP_Y, 0, 0, tiled=True)
     kern, q_parts, col_sum = pl.pallas_call(
         functools.partial(kernel_block, gain),
         out_shape=(
@@ -142,12 +167,12 @@
             jax.ShapeDtypeStruct((n, n, owned), f32),
             jax.ShapeDtypeStruct((1, k_cols), f32),
         ),
-        in_specs=[VMEM] * 2,
+        in_specs=[VMEM] * 3,
         out_specs=(VMEM,) * 3,
         scratch_shapes=[pltpu.VMEM((6 * width + 16, k_cols), bf16)],
         compiler_params=PARAMS,
         name="kernel_block",
-    )(x_feat, y_both)
+    )(held, received, y_both)
     q_parts = lax.all_to_all(q_parts, GROUP_X, 0, 0, tiled=True)
     sums = pl.pallas_call(
         second_block,
@@ -162,16 +187,16 @@
         product_block,
         out_shape=(
             jax.ShapeDtypeStruct((n, block.shape[0], owned), f32),
-            jax.ShapeDtypeStruct((m, 1, owned), f32),
+            jax.ShapeDtypeStruct((1, owned), f32),
         ),
         in_specs=[VMEM] * 3,
         out_specs=(VMEM,) * 2,
+        scratch_shapes=[pltpu.VMEM((m, 1, owned), f32)],
         compiler_params=PARAMS,
         name="product_block",
     )(sums, kern, y_both)
     parts = lax.all_to_all(parts, GROUP_X, 0, 0, tiled=True)
-    own = lax.dynamic_index_in_dim(factor, lax.axis_index(GROUP_Y), 0, keepdims=False)
-    return jnp.sum(parts, axis=0) * own
+    return jnp.sum(parts, axis=0) * factor
 
 
 def solution(mesh):

time: 83.7 us -> 81.4 us (0.973)
  blocking collectives: 35.4 us -> 44.8 us
  waiting for transfers between devices: 17.8 us -> 8.79 us
  local copies, waits for them, and re-layouts: 5.9 us -> 1.41 us
  other arithmetic: 0.63 us -> 2.81 us
  Pallas kernels: 6.96 us -> 5.68 us
  starting transfers between devices: 16.3 us -> 17.2 us
    all_to_all x0 -> x2, blocking collectives: none -> 31.6 us  [the longest x1 20.7 us: per_device(): sums = lax.all_to_all(sums, GROUP_Y, 0, 0, tiled=True)]
    all_gather x1 -> x0, blocking collectives: 21.8 us -> none  [per_device(): y_both = lax.all_gather(both, GROUP_Y)]
    all_to_all x3 -> x1, waiting for transfers between devices: 17.8 us -> 0.01 us  [per_device(): y_both = lax.all_to_all(copies, GROUP_Y, 0, 0, tiled=True)]
    ppermute x0 -> x4, waiting for transfers between devices: none -> 8.78 us  [per_device(): received = lax.ppermute(held, axis, pairs)]
    ppermute x0 -> x4, starting transfers between devices: none -> 5.48 us  [per_device(): received = lax.ppermute(held, axis, pairs)]
    all_to_all x3 -> x1, starting transfers between devices: 16.3 us -> 11.8 us  [per_device(): y_both = lax.all_to_all(copies, GROUP_Y, 0, 0, tiled=True)]
    unnamed x8 -> x4, local copies, waits for them, and re-layouts: 5.89 us -> 1.41 us
    concatenate x0 -> x3, other arithmetic: none -> 2.18 us  [per_device(): held = jnp.concatenate([held, received], axis=0)]
  transfers between devices with their start and end apart: 3 -> 5, of which waited for: 2 -> 4; matrix products, arithmetic and copies ran while one was open for 0% -> 3% of each run, Pallas kernels for 0% -> 0%
where the time goes in v3:
time: 81.4 us; the launch traced here: 80.8 us
  blocking collectives  44.8 us (55%)
  starting transfers between devices  17.2 us (21%)
  waiting for transfers between devices  8.79 us (11%)
  Pallas kernels  5.68 us (7%)
  other arithmetic  2.81 us (3%)
  local copies, waits for them, and re-layouts  1.41 us (2%)
    all_to_all x1, blocking collectives, per_device(): sums = lax.all_to_all(sums, GROUP_Y, 0, 0, tiled=True)  20.7 us
    all_to_all x1, blocking collectives, per_device(): q_parts = lax.all_to_all(q_parts, GROUP_X, 0, 0, tiled=True)  13.2 us
    all_to_all x1, starting transfers between devices, per_device(): y_both = lax.all_to_all(copies, GROUP_Y, 0, 0, tiled=True)  11.8 us
    all_to_all x1, blocking collectives, per_device(): parts = lax.all_to_all(parts, GROUP_X, 0, 0, tiled=True)  10.9 us
    ppermute x4, waiting for transfers between devices, per_device(): received = lax.ppermute(held, axis, pairs)  8.78 us
    ppermute x4, starting transfers between devices, per_device(): received = lax.ppermute(held, axis, pairs)  5.48 us
    pallas_call x1, Pallas kernels, per_device(): pl.pallas_call(functools.partial(kernel_block, gain), out_shape=(jax.Shap...  2.49 us
    concatenate x3, other arithmetic, per_device(): held = jnp.concatenate([held, received], axis=0)  2.18 us
  transfers between devices with their start and end apart: 5, of which 4 were waited for; matrix products, arithmetic and copies ran while one was open for 3% of the time, Pallas kernels for 0%

profile of v3, /device:TPU:1, one launch (start us, length us, event | category | flops | bytes accessed | tf_op | source)
XLA Modules:
  0.0 80.8 jit_solution(7651379700892785527)
XLA Ops:
  0.0 0.0 copy-start
  0.0 0.7 copy-done
  0.7 0.0 copy-start.1
  0.7 0.7 copy-done.1
  1.4 0.8 spread_block.1
  2.2 11.8 %all-to-all-start = ((f32[16,48,96]{2,1,0:T(8,128)}), f32[16,48,96]{2,1,0:T(8,128)S(1)}, u32[]{:S(2)}, u32[]{:S(2)}) async-start(f32[16,48,96]{2,1,0:T(8,128)} %spread_block.1), calls=%async_computation | async-start | bytes 786432 | tf_op jit(solution)/shard_map/all_to_all | solution.py:162
  14.0 1.0 %collective-permute-start = (f32[1,32,96]{2,1,0:T(8,128)}, f32[1,32,96]{2,1,0:T(8,128)S(1)}, u32[]{:S(2)}, u32[]{:S(2)}) collective-permute-start(f32[1,32,96]{2,1,0:T(8,128)} %bitcast.2), channel_id=1, source_target_pairs={{0,1},{1,0},{2,3},{3,2},{4,5},{5,4},{6,7},{7,6},{8,9},{9,8},{10,11... | collective-permute-start | bytes 36872 | tf_op jit(solution)/shard_map/ppermute | solution.py:148
  15.0 1.0 %collective-permute-done = f32[1,32,96]{2,1,0:T(8,128)S(1)} collective-permute-done((f32[1,32,96]{2,1,0:T(8,128)}, f32[1,32,96]{2,1,0:T(8,128)S(1)}, u32[]{:S(2)}, u32[]{:S(2)}) %collective-permute-start) | collective-permute-done | bytes 12320 | tf_op jit(solution)/shard_map/ppermute | solution.py:148
  16.1 0.7 pad_maximum_fusion.2
  16.8 1.2 %collective-permute-start.1 = (f32[2,32,96]{2,1,0:T(8,128)S(1)}, f32[2,32,96]{2,1,0:T(8,128)S(1)}, u32[]{:S(2)}, u32[]{:S(2)}) collective-permute-start(f32[2,32,96]{2,1,0:T(8,128)S(1)} %pad_maximum_fusion.2), channel_id=1, source_target_pairs={{0,2},{2,0},{4,6},{6,4},{1,3},{3,1},{5,7},{7,5},{8,10},{10,8},{12,... | collective-permute-start | bytes 73736 | tf_op jit(solution)/shard_map/ppermute | solution.py:148
  18.0 1.8 %collective-permute-done.1 = f32[2,32,96]{2,1,0:T(8,128)S(1)} collective-permute-done((f32[2,32,96]{2,1,0:T(8,128)S(1)}, f32[2,32,96]{2,1,0:T(8,128)S(1)}, u32[]{:S(2)}, u32[]{:S(2)}) %collective-permute-start.1) | collective-permute-done | bytes 24608 | tf_op jit(solution)/shard_map/ppermute | solution.py:148
  19.9 0.7 pad_maximum_fusion.1
  20.6 2.7 %collective-permute-start.2 = (f32[4,32,96]{2,1,0:T(8,128)S(1)}, f32[4,32,96]{2,1,0:T(8,128)S(1)}, u32[]{:S(2)}, u32[]{:S(2)}) collective-permute-start(f32[4,32,96]{2,1,0:T(8,128)S(1)} %pad_maximum_fusion.1), channel_id=1, source_target_pairs={{0,4},{2,6},{4,0},{6,2},{1,5},{3,7},{5,1},{7,3},{8,12},{10,14},{12... | collective-permute-start | bytes 147464 | tf_op jit(solution)/shard_map/ppermute | solution.py:148
  23.3 2.2 %collective-permute-done.2 = f32[4,32,96]{2,1,0:T(8,128)S(1)} collective-permute-done((f32[4,32,96]{2,1,0:T(8,128)S(1)}, f32[4,32,96]{2,1,0:T(8,128)S(1)}, u32[]{:S(2)}, u32[]{:S(2)}) %collective-permute-start.2) | collective-permute-done | bytes 49184 | tf_op jit(solution)/shard_map/ppermute | solution.py:148
  25.5 0.7 pad_maximum_fusion.near_ref
  26.2 0.5 collective-permute-start.3
  26.7 3.7 %collective-permute-done.3.far_ref = f32[8,32,96]{2,1,0:T(8,128)S(1)} collective-permute-done((f32[8,32,96]{2,1,0:T(8,128)S(1)}, f32[8,32,96]{2,1,0:T(8,128)S(1)}, u32[]{:S(2)}, u32[]{:S(2)}) %collective-permute-start.3) | collective-permute-done | bytes 98336 | tf_op jit(solution)/shard_map/ppermute | solution.py:148
  30.4 0.0 all-to-all-done.y_ref.b_ref
  30.4 2.5 %kernel_block.1 = (bf16[1536,1536]{1,0:T(8,128)(2,1)S(1)}, f32[16,16,96]{2,1,0:T(8,128)S(1)}, f32[1,1536]{1,0:T(1,128)S(1)}) custom-call(f32[8,32,96]{2,1,0:T(8,128)S(1)} %pad_maximum_fusion.near_ref, f32[8,32,96]{2,1,0:T(8,128)S(1)} %collective-permute-done.3.far_ref, f32[16,48,96]{2,1,0:T(8,128)S(1)} %all-to-all-done.y_ref.b_ref), custom_call_target="tpu_custom_call" | custom-call | tf_op jit(solution)/shard_map/kernel_block/pallas_call | solution.py:163
  32.9 13.2 %all_to_all.20.q_ref = f32[16,16,96]{2,1,0:T(8,128)S(1)} all-to-all(f32[16,16,96]{2,1,0:T(8,128)S(1)} %get-tuple-element.10), channel_id=1, replica_groups=mesh['z'=8,'ylo'=2,'yhi'=2,'x'=4,'core'=2] {'ylo','x','core'}, dimensions={0} | all-to-all | bytes 196608 | tf_op jit(solution)/shard_map/all_to_all | solution.py:176
  46.2 1.0 %second_block.1 = f32[16,2,1536]{2,1,0:T(2,128)S(1)} custom-call(f32[16,16,96]{2,1,0:T(8,128)S(1)} %all_to_all.20.q_ref, bf16[1536,1536]{1,0:T(8,128)(2,1)S(1)} %get-tuple-element.11.k_ref, f32[1,1536]{1,0:T(1,128)S(1)} %get-tuple-element.12.col_ref), custom_call_target="tpu_custom_call" | custom-call | tf_op jit(solution)/shard_map/second_block/pallas_call | solution.py:177
  47.2 20.7 %all_to_all.21.m_ref = f32[16,2,1536]{2,1,0:T(2,128)S(1)} all-to-all(f32[16,2,1536]{2,1,0:T(2,128)S(1)} %second_block.1), channel_id=1, replica_groups=mesh['z'=8,'ylo'=2,'yhi'=2,'x'=4,'core'=2] {'z','yhi'}, dimensions={0} | all-to-all | bytes 393216 | tf_op jit(solution)/shard_map/all_to_all | solution.py:185
  67.9 1.4 %product_block.1 = (f32[16,16,96]{2,1,0:T(8,128)S(1)}, f32[1,96]{1,0:T(1,128)S(1)}) custom-call(f32[16,2,1536]{2,1,0:T(2,128)S(1)} %all_to_all.21.m_ref, bf16[1536,1536]{1,0:T(8,128)(2,1)S(1)} %get-tuple-element.11.k_ref, f32[16,48,96]{2,1,0:T(8,128)S(1)} %all-to-all-done.y_ref.b_ref), custom_call_target="tpu_custom_call" | custom-call | tf_op jit(solution)/shard_map/product_block/pallas_call | solution.py:186
  69.3 10.9 %all_to_all.22 = f32[16,16,96]{2,1,0:T(8,128)S(1)} all-to-all(f32[16,16,96]{2,1,0:T(8,128)S(1)} %get-tuple-element.13), channel_id=1, replica_groups=mesh['z'=8,'ylo'=2,'yhi'=2,'x'=4,'core'=2] {'ylo','x','core'}, dimensions={0} | all-to-all | bytes 196608 | tf_op jit(solution)/shard_map/all_to_all | solution.py:198
  80.1 0.6 broadcast_multiply_fusion
  (1 shorter events, 0.0 us)
Async XLA Ops:
  0.0 0.7 copy-start
  0.7 0.7 copy-start.1
  2.2 28.2 %all-to-all-start = ((f32[16,48,96]{2,1,0:T(8,128)}), f32[16,48,96]{2,1,0:T(8,128)S(1)}, u32[]{:S(2)}, u32[]{:S(2)}) async-start(f32[16,48,96]{2,1,0:T(8,128)} %spread_block.1), calls=%async_computation | async-start | bytes 786432 | tf_op jit(solution)/shard_map/all_to_all | solution.py:162
  14.0 2.1 %collective-permute-start = (f32[1,32,96]{2,1,0:T(8,128)}, f32[1,32,96]{2,1,0:T(8,128)S(1)}, u32[]{:S(2)}, u32[]{:S(2)}) collective-permute-start(f32[1,32,96]{2,1,0:T(8,128)} %bitcast.2), channel_id=1, source_target_pairs={{0,1},{1,0},{2,3},{3,2},{4,5},{5,4},{6,7},{7,6},{8,9},{9,8},{10,11... | collective-permute-start | bytes 36872 | tf_op jit(solution)/shard_map/ppermute | solution.py:148
  16.8 3.1 %collective-permute-start.1 = (f32[2,32,96]{2,1,0:T(8,128)S(1)}, f32[2,32,96]{2,1,0:T(8,128)S(1)}, u32[]{:S(2)}, u32[]{:S(2)}) collective-permute-start(f32[2,32,96]{2,1,0:T(8,128)S(1)} %pad_maximum_fusion.2), channel_id=1, source_target_pairs={{0,2},{2,0},{4,6},{6,4},{1,3},{3,1},{5,7},{7,5},{8,10},{10,8},{12,... | collective-permute-start | bytes 73736 | tf_op jit(solution)/shard_map/ppermute | solution.py:148
  20.6 4.9 %collective-permute-start.2 = (f32[4,32,96]{2,1,0:T(8,128)S(1)}, f32[4,32,96]{2,1,0:T(8,128)S(1)}, u32[]{:S(2)}, u32[]{:S(2)}) collective-permute-start(f32[4,32,96]{2,1,0:T(8,128)S(1)} %pad_maximum_fusion.1), channel_id=1, source_target_pairs={{0,4},{2,6},{4,0},{6,2},{1,5},{3,7},{5,1},{7,3},{8,12},{10,14},{12... | collective-permute-start | bytes 147464 | tf_op jit(solution)/shard_map/ppermute | solution.py:148
  26.2 4.2 %collective-permute-start.3 = (f32[8,32,96]{2,1,0:T(8,128)S(1)}, f32[8,32,96]{2,1,0:T(8,128)S(1)}, u32[]{:S(2)}, u32[]{:S(2)}) collective-permute-start(f32[8,32,96]{2,1,0:T(8,128)S(1)} %pad_maximum_fusion.near_ref), channel_id=1, source_target_pairs={{0,16},{16,0},{1,17},{17,1},{2,18},{18,2},{3,19},{19,3},{4,20},{20... | collective-permute-start | bytes 294920 | tf_op jit(solution)/shard_map/ppermute | solution.py:148

commit v4 on v2

--- a/solution.py
+++ b/solution.py
@@ -16,6 +16,13 @@
 ALL = ("z", "ylo", "yhi", "x", "core")
 GROUP_X = ("ylo", "yhi", "x")
 GROUP_Y = ("z", "core")
+
+
+def place_in(axes):
+    place = 0
+    for name in axes:
+        place = place * lax.axis_size(name) + lax.axis_index(name)
+    return place
 
 
 def three_parts(v):
@@ -60,6 +67,7 @@
     col_ref[...] = jnp.zeros_like(col_ref)
     for i in range(count):
         left = extended(x_ref[i] * gain, True)
+        rows = slice(i * width, (i + 1) * width)
         lanes = jnp.zeros((width, 128), f32)
         for j in range(0, total, step):
             expo = lax.dot_general(
@@ -67,7 +75,7 @@
                 preferred_element_type=f32,
             )
             tile = jnp.exp2(expo).astype(bf16)
-            k_ref[i * width : (i + 1) * width, j : j + step] = tile
+            k_ref[rows, j : j + step] = tile
             wide = tile.astype(f32)
             col_ref[:, j : j + step] += jnp.sum(wide, axis=0, keepdims=True)
             for t in range(0, step, 128):
@@ -97,7 +105,7 @@
         out_ref[d, 1:2, :] = second
 
 
-def product_block(m_ref, k_ref, b_ref, out_ref, fac_ref):
+def product_block(m_ref, k_ref, b_ref, out_ref, own_ref, fac_ref):
     count, rows, width = b_ref.shape
     size = rows - out_ref.shape[1]
     sums = jnp.sum(m_ref[...], axis=0)
@@ -111,6 +119,7 @@
             preferred_element_type=f32,
         )
         fac_ref[i] = factor[:, i * width : (i + 1) * width]
+    own_ref[...] = fac_ref[place_in(GROUP_Y)]
 
 
 def per_device(features, block):
@@ -162,16 +171,16 @@
         product_block,
         out_shape=(
             jax.ShapeDtypeStruct((n, block.shape[0], owned), f32),
-            jax.ShapeDtypeStruct((m, 1, owned), f32),
+            jax.ShapeDtypeStruct((1, owned), f32),
         ),
         in_specs=[VMEM] * 3,
         out_specs=(VMEM,) * 2,
+        scratch_shapes=[pltpu.VMEM((m, 1, owned), f32)],
         compiler_params=PARAMS,
         name="product_block",
     )(sums, kern, y_both)
     parts = lax.all_to_all(parts, GROUP_X, 0, 0, tiled=True)
-    own = lax.dynamic_index_in_dim(factor, lax.axis_index(GROUP_Y), 0, keepdims=False)
-    return jnp.sum(parts, axis=0) * own
+    return jnp.sum(parts, axis=0) * factor
 
 
 def solution(mesh):

time: 83.7 us -> 76.6 us (0.915)
  blocking collectives: 35.4 us -> 60.9 us
  waiting for transfers between devices: 17.8 us -> 0.01 us
  starting transfers between devices: 16.3 us -> 7.58 us
  local copies, waits for them, and re-layouts: 5.9 us -> 1.41 us
  Pallas kernels: 6.96 us -> 5.58 us
    all_to_all x0 -> x2, blocking collectives: none -> 25.5 us  [the longest x1 15.3 us: per_device(): sums = lax.all_to_all(sums, GROUP_Y, 0, 0, tiled=True)]
    all_to_all x2 -> x0, waiting for transfers between devices: 17.8 us -> none  [the longest x1 10.3 us: per_device(): sums = lax.all_to_all(sums, GROUP_Y, 0, 0, tiled=True)]
    all_to_all x2 -> x0, starting transfers between devices: 8.74 us -> none  [the longest x1 5.23 us: per_device(): sums = lax.all_to_all(sums, GROUP_Y, 0, 0, tiled=True)]
    unnamed x8 -> x4, local copies, waits for them, and re-layouts: 5.89 us -> 1.41 us
  transfers between devices with their start and end apart: 3 -> 1, of which waited for: 2 -> 0; matrix products, arithmetic and copies ran while one was open for 0% -> 0% of each run, Pallas kernels for 0% -> 0%
where the time goes in v4:
time: 76.6 us; the launch traced here: 76.1 us
  blocking collectives  60.9 us (80%)
  starting transfers between devices  7.58 us (10%)
  Pallas kernels  5.58 us (7%)
  local copies, waits for them, and re-layouts  1.41 us (2%)
    all_gather x1, blocking collectives, per_device(): y_both = lax.all_gather(both, GROUP_Y)  21.8 us
    all_to_all x1, blocking collectives, per_device(): sums = lax.all_to_all(sums, GROUP_Y, 0, 0, tiled=True)  15.3 us
    all_to_all x1, blocking collectives, per_device(): q_parts = lax.all_to_all(q_parts, GROUP_X, 0, 0, tiled=True)  13.6 us
    all_to_all x1, blocking collectives, per_device(): parts = lax.all_to_all(parts, GROUP_X, 0, 0, tiled=True)  10.2 us
    all_to_all x1, starting transfers between devices, per_device(): x_feat = lax.all_to_all(copies, GROUP_X, 0, 0, tiled=True)  7.58 us
    pallas_call x1, Pallas kernels, per_device(): pl.pallas_call(functools.partial(kernel_block, gain), out_shape=(jax.Shap...  2.43 us
  transfers between devices with their start and end apart: 1, of which 0 were waited for; matrix products, arithmetic and copies ran while one was open for 0% of the time, Pallas kernels for 0%

profile of v4, /device:TPU:1, one launch (start us, length us, event | category | flops | bytes accessed | tf_op | source)
XLA Modules:
  0.0 76.1 jit_solution(5369145070139794230)
XLA Ops:
  0.0 0.0 copy-start
  0.0 0.7 copy-done
  0.7 0.0 copy-start.1
  0.7 0.7 copy-done.1
  1.4 0.7 spread_block.1
  2.1 7.6 %all-to-all-start = ((f32[16,32,96]{2,1,0:T(8,128)}), f32[16,32,96]{2,1,0:T(8,128)S(1)}, u32[]{:S(2)}, u32[]{:S(2)}) async-start(f32[16,32,96]{2,1,0:T(8,128)} %get-tuple-element.12), calls=%async_computation | async-start | bytes 524288 | tf_op jit(solution)/shard_map/all_to_all | solution.py:145
  9.7 21.8 %all-gather = f32[768,96]{1,0:T(8,128)S(1)} all-gather(f32[48,96]{1,0:T(8,128)S(1)} %get-tuple-element.13), channel_id=2, replica_groups=mesh['z'=8,'ylo'=2,'yhi'=2,'x'=4,'core'=2] {'z','core'}, dimensions={0}, use_global_device_ids=true | all-gather | bytes 313344 | tf_op jit(solution)/shard_map/all_gather | solution.py:146
  31.6 0.0 all-to-all-done.x_ref
  31.6 2.4 %kernel_block.1 = (bf16[1536,1536]{1,0:T(8,128)(2,1)S(1)}, f32[16,16,96]{2,1,0:T(8,128)S(1)}, f32[1,1536]{1,0:T(1,128)S(1)}) custom-call(f32[16,32,96]{2,1,0:T(8,128)S(1)} %all-to-all-done.x_ref, f32[16,48,96]{2,1,0:T(8,128)S(1)} %bitcast.2), custom_call_target="tpu_custom_call" | custom-call | tf_op jit(solution)/shard_map/kernel_block/pallas_call | solution.py:147
  34.0 13.6 %all_to_all.20.q_ref = f32[16,16,96]{2,1,0:T(8,128)S(1)} all-to-all(f32[16,16,96]{2,1,0:T(8,128)S(1)} %get-tuple-element.14), channel_id=1, replica_groups=mesh['z'=8,'ylo'=2,'yhi'=2,'x'=4,'core'=2] {'ylo','yhi','x'}, dimensions={0} | all-to-all | bytes 196608 | tf_op jit(solution)/shard_map/all_to_all | solution.py:160
  47.6 1.1 %second_block.1 = f32[16,2,1536]{2,1,0:T(2,128)S(1)} custom-call(f32[16,16,96]{2,1,0:T(8,128)S(1)} %all_to_all.20.q_ref, bf16[1536,1536]{1,0:T(8,128)(2,1)S(1)} %get-tuple-element.15.k_ref, f32[1,1536]{1,0:T(1,128)S(1)} %get-tuple-element.16.col_ref), custom_call_target="tpu_custom_call" | custom-call | tf_op jit(solution)/shard_map/second_block/pallas_call | solution.py:161
  48.6 15.3 %all_to_all.21.m_ref = f32[16,2,1536]{2,1,0:T(2,128)S(1)} all-to-all(f32[16,2,1536]{2,1,0:T(2,128)S(1)} %second_block.1), channel_id=1, replica_groups=mesh['z'=8,'ylo'=2,'yhi'=2,'x'=4,'core'=2] {'z','core'}, dimensions={0} | all-to-all | bytes 393216 | tf_op jit(solution)/shard_map/all_to_all | solution.py:169
  64.0 1.4 %product_block.1 = (f32[16,16,96]{2,1,0:T(8,128)S(1)}, f32[1,96]{1,0:T(1,128)S(1)}) custom-call(f32[16,2,1536]{2,1,0:T(2,128)S(1)} %all_to_all.21.m_ref, bf16[1536,1536]{1,0:T(8,128)(2,1)S(1)} %get-tuple-element.15.k_ref, f32[16,48,96]{2,1,0:T(8,128)S(1)} %bitcast.3), custom_call_target="tpu_custom_call" | custom-call | tf_op jit(solution)/shard_map/product_block/pallas_call | solution.py:170
  65.3 10.2 %all_to_all.22 = f32[16,16,96]{2,1,0:T(8,128)S(1)} all-to-all(f32[16,16,96]{2,1,0:T(8,128)S(1)} %get-tuple-element.17), channel_id=1, replica_groups=mesh['z'=8,'ylo'=2,'yhi'=2,'x'=4,'core'=2] {'ylo','yhi','x'}, dimensions={0} | all-to-all | bytes 196608 | tf_op jit(solution)/shard_map/all_to_all | solution.py:182
  75.5 0.6 broadcast_multiply_fusion
  (1 shorter events, 0.0 us)
Async XLA Ops:
  0.0 0.7 copy-start
  0.7 0.7 copy-start.1
  2.1 29.4 %all-to-all-start = ((f32[16,32,96]{2,1,0:T(8,128)}), f32[16,32,96]{2,1,0:T(8,128)S(1)}, u32[]{:S(2)}, u32[]{:S(2)}) async-start(f32[16,32,96]{2,1,0:T(8,128)} %get-tuple-element.12), calls=%async_computation | async-start | bytes 524288 | tf_op jit(solution)/shard_map/all_to_all | solution.py:145

commit v5 on v4

--- a/solution.py
+++ b/solution.py
@@ -49,22 +49,32 @@
     return jnp.concatenate(parts, axis=0)
 
 
-def spread_block(f_ref, b_ref, x_ref, y_ref):
+def spread_block(f_ref, b_ref, x_ref, y_ref, here, in_sem, x_sem, y_sem):
     width = f_ref.shape[0]
-    values = f_ref[...]
-    for i in range(x_ref.shape[0]):
-        x_ref[i] = values
-    y_ref[:width] = values
-    y_ref[width:] = b_ref[...]
-
-
-def kernel_block(gain, x_ref, y_ref, k_ref, q_ref, col_ref, right_ref):
+    fetch = pltpu.make_async_copy(f_ref, here, in_sem)
+    fetch.start()
+    lower = pltpu.make_async_copy(f_ref, y_ref.at[pl.ds(0, width)], y_sem.at[0])
+    upper = pltpu.make_async_copy(b_ref, y_ref.at[pl.ds(width, b_ref.shape[0])], y_sem.at[1])
+    lower.start()
+    upper.start()
+    fetch.wait()
+    copies = [
+        pltpu.make_async_copy(here, x_ref.at[i], x_sem.at[i]) for i in range(x_ref.shape[0])
+    ]
+    for copy in copies:
+        copy.start()
+    for copy in copies:
+        copy.wait()
+    lower.wait()
+    upper.wait()
+
+
+def kernel_block(gain, x_ref, y_ref, k_ref, q_ref, right_ref):
     count, size, width = x_ref.shape
     total = k_ref.shape[1]
     y = jnp.concatenate([y_ref[i, :size] for i in range(count)], axis=1) * gain
     right_ref[...] = extended(y, False)
     step = 512
-    col_ref[...] = jnp.zeros_like(col_ref)
     for i in range(count):
         left = extended(x_ref[i] * gain, True)
         rows = slice(i * width, (i + 1) * width)
@@ -77,7 +87,6 @@
             tile = jnp.exp2(expo).astype(bf16)
             k_ref[rows, j : j + step] = tile
             wide = tile.astype(f32)
-            col_ref[:, j : j + step] += jnp.sum(wide, axis=0, keepdims=True)
             for t in range(0, step, 128):
                 lanes = lanes + wide[:, t : t + 128]
         sums = jnp.sum(lanes.T, axis=0, keepdims=True)
@@ -85,10 +94,14 @@
             q_ref[d, i : i + 1, :] = sums
 
 
-def second_block(q_ref, k_ref, col_ref, out_ref):
+def second_block(q_ref, k_ref, out_ref, sum_ref, line_ref):
+    line_ref[...] = jnp.zeros_like(line_ref)
     count, _, width = q_ref.shape
     total = k_ref.shape[1]
-    inv = 1.0 / jnp.sum(q_ref[...], axis=0)
+    q = jnp.sum(q_ref[...], axis=0)
+    sum_ref[...] = q
+    own = sum_ref[pl.ds(place_in(GROUP_X), 1), :]
+    inv = 1.0 / q
     acc = jnp.zeros((8, total), f32)
     for i in range(count):
         tall = jnp.broadcast_to(inv[i : i + 1, :], (128, width)).T
@@ -100,26 +113,60 @@
             )
             acc = acc + prod[:8] + prod[8:]
     second = jnp.sum(acc, axis=0, keepdims=True)
-    for d in range(count):
-        out_ref[d, 0:1, :] = col_ref[...]
-        out_ref[d, 1:2, :] = second
-
-
-def product_block(m_ref, k_ref, b_ref, out_ref, own_ref, fac_ref):
+    mine = place_in(GROUP_Y)
+    second = second - jnp.concatenate(
+        [jnp.where(mine == i, 1.0 / own, 0.0) for i in range(total // width)], axis=1
+    )
+    second = second * (1.0 + mine.astype(f32) / out_ref.shape[0])
+    lines = total // 128
+    for i in range(lines):
+        line_ref[i : i + 1, :] = second[:, i * 128 : (i + 1) * 128]
+    for i, part in enumerate(three_parts(own)):
+        line_ref[lines + i : lines + i + 1, :width] = part.astype(f32)
+    message = line_ref[...].astype(bf16)
+    for d in range(out_ref.shape[0]):
+        out_ref[d] = message
+
+
+def product_block(m_ref, k_ref, b_ref, out_ref, own_ref, add_ref, fac_ref, line_ref):
     count, rows, width = b_ref.shape
     size = rows - out_ref.shape[1]
-    sums = jnp.sum(m_ref[...], axis=0)
-    inv = 1.0 / sums[0:1]
-    factor = inv * lax.rsqrt(sums[1:2] * inv)
+    lines = k_ref.shape[1] // 128
+    summed = m_ref[0].astype(f32)
+    line_ref[0] = summed
+    for i in range(1, count):
+        lined = m_ref[i].astype(f32)
+        line_ref[i] = lined
+        summed = summed + lined * (1.0 / (1.0 + i / count))
+    q = jnp.concatenate(
+        [
+            line_ref[i, lines : lines + 1, :width]
+            + line_ref[i, lines + 1 : lines + 2, :width]
+            + line_ref[i, lines + 2 : lines + 3, :width]
+            for i in range(count)
+        ],
+        axis=1,
+    )
+    line_ref[0] = summed
+    second = jnp.concatenate([line_ref[0, i : i + 1, :] for i in range(lines)], axis=1)
+    inv = 1.0 / q
+    second = second + inv
+    factor = inv * lax.rsqrt(second * inv)
     block = jnp.concatenate([b_ref[i, size:] for i in range(count)], axis=1)
     weighted = (block * factor).astype(bf16)
     for i in range(count):
-        out_ref[i] = lax.dot_general(
+        fac_ref[i] = factor[:, i * width : (i + 1) * width]
+    place, mine = place_in(GROUP_X), place_in(GROUP_Y)
+    own = fac_ref[mine]
+    own_ref[...] = own
+    added = (b_ref[mine, size:] * own).astype(bf16).astype(f32)
+    add_ref[...] = added
+    for i in range(out_ref.shape[0]):
+        value = lax.dot_general(
             weighted, k_ref[i * width : (i + 1) * width, :], (((1,), (1,)), ((), ())),
             preferred_element_type=f32,
         )
-        fac_ref[i] = factor[:, i * width : (i + 1) * width]
-    own_ref[...] = fac_ref[place_in(GROUP_Y)]
+        out_ref[i] = jnp.where(place == i, value - added, value).astype(bf16)
 
 
 def per_device(features, block):
@@ -130,29 +177,37 @@
     scale = 4.0 / (float(frames) ** (2.0 / width) - 1.0)
     gain = math.sqrt(2.0 * math.log2(math.e) / scale)
     k_rows, k_cols = n * owned, m * owned
-
+    lines = pl.cdiv(k_cols // 128 + 3, 16) * 16
+
+    anywhere = pl.BlockSpec(memory_space=pl.ANY)
     copies, both = pl.pallas_call(
         spread_block,
         out_shape=(
             jax.ShapeDtypeStruct((n, width, owned), f32),
             jax.ShapeDtypeStruct((width + block.shape[0], owned), f32),
         ),
-        in_specs=[VMEM] * 2,
-        out_specs=(VMEM,) * 2,
+        in_specs=[anywhere] * 2,
+        out_specs=(anywhere,) * 2,
+        scratch_shapes=[
+            pltpu.VMEM((width, owned), f32),
+            pltpu.SemaphoreType.DMA,
+            pltpu.SemaphoreType.DMA((n,)),
+            pltpu.SemaphoreType.DMA((2,)),
+        ],
+        cost_estimate=pl.CostEstimate(flops=0, bytes_accessed=0, transcendentals=0),
         compiler_params=PARAMS,
         name="spread_block",
-    )(features, block)
+    )(*(pltpu.with_memory_space_constraint(a, pltpu.HBM) for a in (features, block)))
     x_feat = lax.all_to_all(copies, GROUP_X, 0, 0, tiled=True)
     y_both = lax.all_gather(both, GROUP_Y)
-    kern, q_parts, col_sum = pl.pallas_call(
+    kern, q_parts = pl.pallas_call(
         functools.partial(kernel_block, gain),
         out_shape=(
             jax.ShapeDtypeStruct((k_rows, k_cols), bf16),
             jax.ShapeDtypeStruct((n, n, owned), f32),
-            jax.ShapeDtypeStruct((1, k_cols), f32),
         ),
         in_specs=[VMEM] * 2,
-        out_specs=(VMEM,) * 3,
+        out_specs=(VMEM,) * 2,
         scratch_shapes=[pltpu.VMEM((6 * width + 16, k_cols), bf16)],
         compiler_params=PARAMS,
         name="kernel_block",
@@ -160,27 +215,29 @@
     q_parts = lax.all_to_all(q_parts, GROUP_X, 0, 0, tiled=True)
     sums = pl.pallas_call(
         second_block,
-        out_shape=jax.ShapeDtypeStruct((m, 2, k_cols), f32),
-        in_specs=[VMEM] * 3,
+        out_shape=jax.ShapeDtypeStruct((m, lines, 128), bf16),
+        in_specs=[VMEM] * 2,
         out_specs=VMEM,
+        scratch_shapes=[pltpu.VMEM((n, owned), f32), pltpu.VMEM((lines, 128), f32)],
         compiler_params=PARAMS,
         name="second_block",
-    )(q_parts, kern, col_sum)
+    )(q_parts, kern)
     sums = lax.all_to_all(sums, GROUP_Y, 0, 0, tiled=True)
-    parts, factor = pl.pallas_call(
+    parts, factor, diagonal = pl.pallas_call(
         product_block,
         out_shape=(
-            jax.ShapeDtypeStruct((n, block.shape[0], owned), f32),
+            jax.ShapeDtypeStruct((n, block.shape[0], owned), bf16),
             jax.ShapeDtypeStruct((1, owned), f32),
+            jax.ShapeDtypeStruct(block.shape, f32),
         ),
         in_specs=[VMEM] * 3,
-        out_specs=(VMEM,) * 2,
-        scratch_shapes=[pltpu.VMEM((m, 1, owned), f32)],
+        out_specs=(VMEM,) * 3,
+        scratch_shapes=[pltpu.VMEM((m, 1, owned), f32), pltpu.VMEM((m, lines, 128), f32)],
         compiler_params=PARAMS,
         name="product_block",
     )(sums, kern, y_both)
     parts = lax.all_to_all(parts, GROUP_X, 0, 0, tiled=True)
-    return jnp.sum(parts, axis=0) * factor
+    return (jnp.sum(parts.astype(f32), axis=0) + diagonal) * factor
 
 
 def solution(mesh):

time: 76.6 us -> 72 us (0.940)
  blocking collectives: 60.9 us -> 57.5 us
  local copies, waits for them, and re-layouts: 1.41 us -> 0 us
    all_to_all x1, blocking collectives: 15.3 us -> 12.8 us  [per_device(): sums = lax.all_to_all(sums, GROUP_Y, 0, 0, tiled=True)]
    unnamed x4 -> x0, local copies, waits for them, and re-layouts: 1.41 us -> none
    pallas_call x1, Pallas kernels: 0.72 us -> 1.65 us  [per_device(): pl.pallas_call(spread_block, out_shape=(jax.ShapeDtypeStruct((n, width, o...]
    all_to_all x1, blocking collectives: 10.2 us -> 9.25 us  [per_device(): parts = lax.all_to_all(parts, GROUP_X, 0, 0, tiled=True)]
where the time goes in v5:
time: 72 us; the launch traced here: 71.7 us
  blocking collectives  57.5 us (80%)
  starting transfers between devices  7.6 us (11%)
  Pallas kernels  5.94 us (8%)
    all_gather x1, blocking collectives, per_device(): y_both = lax.all_gather(both, GROUP_Y)  21.8 us
    all_to_all x1, blocking collectives, per_device(): q_parts = lax.all_to_all(q_parts, GROUP_X, 0, 0, tiled=True)  13.6 us
    all_to_all x1, blocking collectives, per_device(): sums = lax.all_to_all(sums, GROUP_Y, 0, 0, tiled=True)  12.8 us
    all_to_all x1, blocking collectives, per_device(): parts = lax.all_to_all(parts, GROUP_X, 0, 0, tiled=True)  9.25 us
    all_to_all x1, starting transfers between devices, per_device(): x_feat = lax.all_to_all(copies, GROUP_X, 0, 0, tiled=True)  7.6 us
    pallas_call x1, Pallas kernels, per_device(): pl.pallas_call(functools.partial(kernel_block, gain), out_shape=(jax.Shap...  1.84 us
    pallas_call x1, Pallas kernels, per_device(): pl.pallas_call(spread_block, out_shape=(jax.ShapeDtypeStruct((n, width, o...  1.65 us
  transfers between devices with their start and end apart: 1, of which 0 were waited for; matrix products, arithmetic and copies ran while one was open for 0% of the time, Pallas kernels for 0%

profile of v5, /device:TPU:1, one launch (start us, length us, event | category | flops | bytes accessed | tf_op | source)
XLA Modules:
  0.0 71.7 jit_solution(14821060339255205750)
XLA Ops:
  0.0 1.6 %spread_block.1 = (f32[16,32,96]{2,1,0:T(8,128)}, f32[48,96]{1,0:T(8,128)S(1)}) custom-call(f32[32,96]{1,0:T(8,128)} %f_ref.1, f32[16,96]{1,0:T(8,128)} %b_ref.1), custom_call_target="tpu_custom_call" | custom-call | tf_op jit(solution)/shard_map/spread_block/pallas_call | solution.py:183
  1.7 7.6 %all-to-all-start = ((f32[16,32,96]{2,1,0:T(8,128)}), f32[16,32,96]{2,1,0:T(8,128)S(1)}, u32[]{:S(2)}, u32[]{:S(2)}) async-start(f32[16,32,96]{2,1,0:T(8,128)} %get-tuple-element.12), calls=%async_computation | async-start | bytes 524288 | tf_op jit(solution)/shard_map/all_to_all | solution.py:201
  9.3 21.8 %all-gather = f32[768,96]{1,0:T(8,128)S(1)} all-gather(f32[48,96]{1,0:T(8,128)S(1)} %get-tuple-element.13), channel_id=2, replica_groups=mesh['z'=8,'ylo'=2,'yhi'=2,'x'=4,'core'=2] {'z','core'}, dimensions={0}, use_global_device_ids=true | all-gather | bytes 313344 | tf_op jit(solution)/shard_map/all_gather | solution.py:202
  31.1 0.0 all-to-all-done.x_ref
  31.1 1.8 %kernel_block.1 = (bf16[1536,1536]{1,0:T(8,128)(2,1)S(1)}, f32[16,16,96]{2,1,0:T(8,128)S(1)}) custom-call(f32[16,32,96]{2,1,0:T(8,128)S(1)} %all-to-all-done.x_ref, f32[16,48,96]{2,1,0:T(8,128)S(1)} %bitcast.2), custom_call_target="tpu_custom_call" | custom-call | tf_op jit(solution)/shard_map/kernel_block/pallas_call | solution.py:203
  32.9 13.6 %all_to_all.20.q_ref = f32[16,16,96]{2,1,0:T(8,128)S(1)} all-to-all(f32[16,16,96]{2,1,0:T(8,128)S(1)} %get-tuple-element.14), channel_id=1, replica_groups=mesh['z'=8,'ylo'=2,'yhi'=2,'x'=4,'core'=2] {'ylo','yhi','x'}, dimensions={0} | all-to-all | bytes 196608 | tf_op jit(solution)/shard_map/all_to_all | solution.py:215
  46.5 1.1 %second_block.1 = bf16[16,16,128]{2,1,0:T(8,128)(2,1)S(1)} custom-call(f32[16,16,96]{2,1,0:T(8,128)S(1)} %all_to_all.20.q_ref, bf16[1536,1536]{1,0:T(8,128)(2,1)S(1)} %get-tuple-element.15.k_ref), custom_call_target="tpu_custom_call" | custom-call | tf_op jit(solution)/shard_map/second_block/pallas_call | solution.py:216
  47.6 12.8 %all_to_all.21.m_ref = bf16[16,16,128]{2,1,0:T(8,128)(2,1)S(1)} all-to-all(bf16[16,16,128]{2,1,0:T(8,128)(2,1)S(1)} %second_block.1), channel_id=1, replica_groups=mesh['z'=8,'ylo'=2,'yhi'=2,'x'=4,'core'=2] {'z','core'}, dimensions={0} | all-to-all | bytes 131072 | tf_op jit(solution)/shard_map/all_to_all | solution.py:225
  60.4 1.4 %product_block.1 = (bf16[16,16,96]{2,1,0:T(8,128)(2,1)S(1)}, f32[1,96]{1,0:T(1,128)S(1)}, f32[16,96]{1,0:T(8,128)S(1)}) custom-call(bf16[16,16,128]{2,1,0:T(8,128)(2,1)S(1)} %all_to_all.21.m_ref, bf16[1536,1536]{1,0:T(8,128)(2,1)S(1)} %get-tuple-element.15.k_ref, f32[16,48,96]{2,1,0:T(8,128)S(1)} %bitcast.3), custom_call_target="tpu_custom_call" | custom-call | tf_op jit(solution)/shard_map/product_block/pallas_call | solution.py:226
  61.8 9.2 %all_to_all.22 = bf16[16,16,96]{2,1,0:T(8,128)(2,1)S(1)} all-to-all(bf16[16,16,96]{2,1,0:T(8,128)(2,1)S(1)} %get-tuple-element.16), channel_id=1, replica_groups=mesh['z'=8,'ylo'=2,'yhi'=2,'x'=4,'core'=2] {'ylo','yhi','x'}, dimensions={0} | all-to-all | bytes 98304 | tf_op jit(solution)/shard_map/all_to_all | solution.py:239
  71.1 0.6 add_multiply_fusion
  (1 shorter events, 0.0 us)
Async XLA Ops:
  1.7 29.4 %all-to-all-start = ((f32[16,32,96]{2,1,0:T(8,128)}), f32[16,32,96]{2,1,0:T(8,128)S(1)}, u32[]{:S(2)}, u32[]{:S(2)}) async-start(f32[16,32,96]{2,1,0:T(8,128)} %get-tuple-element.12), calls=%async_computation | async-start | bytes 524288 | tf_op jit(solution)/shard_map/all_to_all | solution.py:201

commit v6 on v5

--- a/solution.py
+++ b/solution.py
@@ -72,55 +72,57 @@
 def kernel_block(gain, x_ref, y_ref, k_ref, q_ref, right_ref):
     count, size, width = x_ref.shape
     total = k_ref.shape[1]
-    y = jnp.concatenate([y_ref[i, :size] for i in range(count)], axis=1) * gain
-    right_ref[...] = extended(y, False)
+    x = jnp.concatenate([x_ref[i] for i in range(count)], axis=1) * gain
+    right_ref[...] = extended(x, False)
     step = 512
-    for i in range(count):
-        left = extended(x_ref[i] * gain, True)
-        rows = slice(i * width, (i + 1) * width)
-        lanes = jnp.zeros((width, 128), f32)
+    sums = [jnp.zeros((8, step), f32) for _ in range(0, total, step)]
+    for i in range(y_ref.shape[0]):
+        left = extended(y_ref[i, :size] * gain, True)
         for j in range(0, total, step):
             expo = lax.dot_general(
                 left, right_ref[:, j : j + step], (((0,), (0,)), ((), ())),
                 preferred_element_type=f32,
             )
             tile = jnp.exp2(expo).astype(bf16)
-            k_ref[rows, j : j + step] = tile
+            k_ref[i * width : (i + 1) * width, j : j + step] = tile
             wide = tile.astype(f32)
-            for t in range(0, step, 128):
-                lanes = lanes + wide[:, t : t + 128]
-        sums = jnp.sum(lanes.T, axis=0, keepdims=True)
-        for d in range(count):
-            q_ref[d, i : i + 1, :] = sums
+            part = sums[j // step]
+            for r in range(0, width, 8):
+                part = part + wide[r : r + 8]
+            sums[j // step] = part
+    flat = jnp.sum(jnp.concatenate(sums, axis=1), axis=0, keepdims=True)
+    for d in range(q_ref.shape[0]):
+        q_ref[d] = flat
 
 
 def second_block(q_ref, k_ref, out_ref, sum_ref, line_ref):
     line_ref[...] = jnp.zeros_like(line_ref)
-    count, _, width = q_ref.shape
-    total = k_ref.shape[1]
-    q = jnp.sum(q_ref[...], axis=0)
-    sum_ref[...] = q
-    own = sum_ref[pl.ds(place_in(GROUP_X), 1), :]
+    count, _, total = q_ref.shape
+    width = sum_ref.shape[2]
+    q = q_ref[0]
+    for i in range(1, count):
+        q = q + q_ref[i]
+    for i in range(count):
+        sum_ref[i] = q[:, i * width : (i + 1) * width]
+    own = sum_ref[place_in(GROUP_X)]
     inv = 1.0 / q
-    acc = jnp.zeros((8, total), f32)
-    for i in range(count):
-        tall = jnp.broadcast_to(inv[i : i + 1, :], (128, width)).T
-        for r in range(0, width, 16):
-            rows = k_ref[i * width + r : i * width + r + 16, :].astype(f32)
-            w = tall[r : r + 16, :]
-            prod = jnp.concatenate(
-                [rows[:, t : t + 128] * w for t in range(0, total, 128)], axis=1
-            )
-            acc = acc + prod[:8] + prod[8:]
-    second = jnp.sum(acc, axis=0, keepdims=True)
+    pieces = [jnp.broadcast_to(inv[:, t : t + 128], (16, 128)) for t in range(0, total, 128)]
     mine = place_in(GROUP_Y)
-    second = second - jnp.concatenate(
-        [jnp.where(mine == i, 1.0 / own, 0.0) for i in range(total // width)], axis=1
-    )
-    second = second * (1.0 + mine.astype(f32) / out_ref.shape[0])
-    lines = total // 128
+    apart = jnp.concatenate(
+        [jnp.where(mine == i, 1.0 / own, 0.0) for i in range(k_ref.shape[0] // width)], axis=1
+    )
+    grade = 1.0 + mine.astype(f32) / out_ref.shape[0]
+    lines = k_ref.shape[0] // 128
     for i in range(lines):
-        line_ref[i : i + 1, :] = second[:, i * 128 : (i + 1) * 128]
+        groups = []
+        for r in range(0, 128, 16):
+            acc = jnp.zeros((16, 128), f32)
+            for t, piece in enumerate(pieces):
+                rows = k_ref[i * 128 + r : i * 128 + r + 16, t * 128 : (t + 1) * 128]
+                acc = acc + rows.astype(f32) * piece
+            groups.append(acc)
+        line = jnp.sum(jnp.concatenate(groups, axis=0).T, axis=0, keepdims=True)
+        line_ref[i : i + 1, :] = (line - apart[:, i * 128 : (i + 1) * 128]) * grade
     for i, part in enumerate(three_parts(own)):
         line_ref[lines + i : lines + i + 1, :width] = part.astype(f32)
     message = line_ref[...].astype(bf16)
@@ -131,7 +133,7 @@
 def product_block(m_ref, k_ref, b_ref, out_ref, own_ref, add_ref, fac_ref, line_ref):
     count, rows, width = b_ref.shape
     size = rows - out_ref.shape[1]
-    lines = k_ref.shape[1] // 128
+    lines = k_ref.shape[0] // 128
     summed = m_ref[0].astype(f32)
     line_ref[0] = summed
     for i in range(1, count):
@@ -161,11 +163,16 @@
     own_ref[...] = own
     added = (b_ref[mine, size:] * own).astype(bf16).astype(f32)
     add_ref[...] = added
+    step = 512
+    values = jnp.concatenate(
+        [
+            jnp.dot(weighted, k_ref[:, j : j + step], preferred_element_type=f32)
+            for j in range(0, k_ref.shape[1], step)
+        ],
+        axis=1,
+    )
     for i in range(out_ref.shape[0]):
-        value = lax.dot_general(
-            weighted, k_ref[i * width : (i + 1) * width, :], (((1,), (1,)), ((), ())),
-            preferred_element_type=f32,
-        )
+        value = values[:, i * width : (i + 1) * width]
         out_ref[i] = jnp.where(place == i, value - added, value).astype(bf16)
 
 
@@ -176,8 +183,8 @@
     frames = owned * n * m
     scale = 4.0 / (float(frames) ** (2.0 / width) - 1.0)
     gain = math.sqrt(2.0 * math.log2(math.e) / scale)
-    k_rows, k_cols = n * owned, m * owned
-    lines = pl.cdiv(k_cols // 128 + 3, 16) * 16
+    x_total, y_total = n * owned, m * owned
+    lines = pl.cdiv(y_total // 128 + 3, 16) * 16
 
     anywhere = pl.BlockSpec(memory_space=pl.ANY)
     copies, both = pl.pallas_call(
@@ -203,12 +210,12 @@
     kern, q_parts = pl.pallas_call(
         functools.partial(kernel_block, gain),
         out_shape=(
-            jax.ShapeDtypeStruct((k_rows, k_cols), bf16),
-            jax.ShapeDtypeStruct((n, n, owned), f32),
+            jax.ShapeDtypeStruct((y_total, x_total), bf16),
+            jax.ShapeDtypeStruct((n, 1, x_total), f32),
         ),
         in_specs=[VMEM] * 2,
         out_specs=(VMEM,) * 2,
-        scratch_shapes=[pltpu.VMEM((6 * width + 16, k_cols), bf16)],
+        scratch_shapes=[pltpu.VMEM((6 * width + 16, x_total), bf16)],
         compiler_params=PARAMS,
         name="kernel_block",
     )(x_feat, y_both)
@@ -218,7 +225,7 @@
         out_shape=jax.ShapeDtypeStruct((m, lines, 128), bf16),
         in_specs=[VMEM] * 2,
         out_specs=VMEM,
-        scratch_shapes=[pltpu.VMEM((n, owned), f32), pltpu.VMEM((lines, 128), f32)],
+        scratch_shapes=[pltpu.VMEM((n, 1, owned), f32), pltpu.VMEM((lines, 128), f32)],
         compiler_params=PARAMS,
         name="second_block",
     )(q_parts, kern)

time: 72 us -> 71.5 us (level)
  no operation moved by 1% of the time
where the time goes in v6:
time: 71.5 us; the launch traced here: 71.2 us
  blocking collectives  57.4 us (80%)
  starting transfers between devices  7.6 us (11%)
  Pallas kernels  5.53 us (8%)
    all_gather x1, blocking collectives, per_device(): y_both = lax.all_gather(both, GROUP_Y)  21.8 us
    all_to_all x1, blocking collectives, per_device(): q_parts = lax.all_to_all(q_parts, GROUP_X, 0, 0, tiled=True)  13.4 us
    all_to_all x1, blocking collectives, per_device(): sums = lax.all_to_all(sums, GROUP_Y, 0, 0, tiled=True)  12.8 us
    all_to_all x1, blocking collectives, per_device(): parts = lax.all_to_all(parts, GROUP_X, 0, 0, tiled=True)  9.31 us
    all_to_all x1, starting transfers between devices, per_device(): x_feat = lax.all_to_all(copies, GROUP_X, 0, 0, tiled=True)  7.6 us
    pallas_call x1, Pallas kernels, per_device(): pl.pallas_call(functools.partial(kernel_block, gain), out_shape=(jax.Shap...  1.99 us
    pallas_call x1, Pallas kernels, per_device(): pl.pallas_call(spread_block, out_shape=(jax.ShapeDtypeStruct((n, width, o...  1.65 us
  transfers between devices with their start and end apart: 1, of which 0 were waited for; matrix products, arithmetic and copies ran while one was open for 0% of the time, Pallas kernels for 0%

profile of v6, /device:TPU:1, one launch (start us, length us, event | category | flops | bytes accessed | tf_op | source)
XLA Modules:
  0.0 71.2 jit_solution(3405349831600663998)
XLA Ops:
  0.0 1.6 %spread_block.1 = (f32[16,32,96]{2,1,0:T(8,128)}, f32[48,96]{1,0:T(8,128)S(1)}) custom-call(f32[32,96]{1,0:T(8,128)} %f_ref.1, f32[16,96]{1,0:T(8,128)} %b_ref.1), custom_call_target="tpu_custom_call" | custom-call | tf_op jit(solution)/shard_map/spread_block/pallas_call | solution.py:190
  1.7 7.6 %all-to-all-start = ((f32[16,32,96]{2,1,0:T(8,128)}), f32[16,32,96]{2,1,0:T(8,128)S(1)}, u32[]{:S(2)}, u32[]{:S(2)}) async-start(f32[16,32,96]{2,1,0:T(8,128)} %get-tuple-element.12), calls=%async_computation | async-start | bytes 524288 | tf_op jit(solution)/shard_map/all_to_all | solution.py:208
  9.3 21.8 %all-gather = f32[768,96]{1,0:T(8,128)S(1)} all-gather(f32[48,96]{1,0:T(8,128)S(1)} %get-tuple-element.13), channel_id=2, replica_groups=mesh['z'=8,'ylo'=2,'yhi'=2,'x'=4,'core'=2] {'z','core'}, dimensions={0}, use_global_device_ids=true | all-gather | bytes 313344 | tf_op jit(solution)/shard_map/all_gather | solution.py:209
  31.1 0.0 all-to-all-done.x_ref
  31.1 2.0 %kernel_block.1 = (bf16[1536,1536]{1,0:T(8,128)(2,1)S(1)}, f32[16,1,1536]{2,1,0:T(1,128)S(1)}) custom-call(f32[16,32,96]{2,1,0:T(8,128)S(1)} %all-to-all-done.x_ref, f32[16,48,96]{2,1,0:T(8,128)S(1)} %bitcast.2), custom_call_target="tpu_custom_call" | custom-call | tf_op jit(solution)/shard_map/kernel_block/pallas_call | solution.py:210
  33.1 13.4 %all_to_all.20.q_ref = f32[16,1,1536]{2,1,0:T(1,128)S(1)} all-to-all(f32[16,1,1536]{2,1,0:T(1,128)S(1)} %get-tuple-element.14), channel_id=1, replica_groups=mesh['z'=8,'ylo'=2,'yhi'=2,'x'=4,'core'=2] {'ylo','yhi','x'}, dimensions={0} | all-to-all | bytes 196608 | tf_op jit(solution)/shard_map/all_to_all | solution.py:222
  46.5 1.0 %second_block.1 = bf16[16,16,128]{2,1,0:T(8,128)(2,1)S(1)} custom-call(f32[16,1,1536]{2,1,0:T(1,128)S(1)} %all_to_all.20.q_ref, bf16[1536,1536]{1,0:T(8,128)(2,1)S(1)} %get-tuple-element.15.k_ref), custom_call_target="tpu_custom_call" | custom-call | tf_op jit(solution)/shard_map/second_block/pallas_call | solution.py:223
  47.5 12.8 %all_to_all.21.m_ref = bf16[16,16,128]{2,1,0:T(8,128)(2,1)S(1)} all-to-all(bf16[16,16,128]{2,1,0:T(8,128)(2,1)S(1)} %second_block.1), channel_id=1, replica_groups=mesh['z'=8,'ylo'=2,'yhi'=2,'x'=4,'core'=2] {'z','core'}, dimensions={0} | all-to-all | bytes 131072 | tf_op jit(solution)/shard_map/all_to_all | solution.py:232
  60.4 0.9 %product_block.1 = (bf16[16,16,96]{2,1,0:T(8,128)(2,1)S(1)}, f32[1,96]{1,0:T(1,128)S(1)}, f32[16,96]{1,0:T(8,128)S(1)}) custom-call(bf16[16,16,128]{2,1,0:T(8,128)(2,1)S(1)} %all_to_all.21.m_ref, bf16[1536,1536]{1,0:T(8,128)(2,1)S(1)} %get-tuple-element.15.k_ref, f32[16,48,96]{2,1,0:T(8,128)S(1)} %bitcast.3), custom_call_target="tpu_custom_call" | custom-call | tf_op jit(solution)/shard_map/product_block/pallas_call | solution.py:233
  61.2 9.3 %all_to_all.22 = bf16[16,16,96]{2,1,0:T(8,128)(2,1)S(1)} all-to-all(bf16[16,16,96]{2,1,0:T(8,128)(2,1)S(1)} %get-tuple-element.16), channel_id=1, replica_groups=mesh['z'=8,'ylo'=2,'yhi'=2,'x'=4,'core'=2] {'ylo','yhi','x'}, dimensions={0} | all-to-all | bytes 98304 | tf_op jit(solution)/shard_map/all_to_all | solution.py:246
  70.6 0.6 add_multiply_fusion
  (1 shorter events, 0.0 us)
Async XLA Ops:
  1.7 29.4 %all-to-all-start = ((f32[16,32,96]{2,1,0:T(8,128)}), f32[16,32,96]{2,1,0:T(8,128)S(1)}, u32[]{:S(2)}, u32[]{:S(2)}) async-start(f32[16,32,96]{2,1,0:T(8,128)} %get-tuple-element.12), calls=%async_computation | async-start | bytes 524288 | tf_op jit(solution)/shard_map/all_to_all | solution.py:208

commit v7 on v6

--- a/solution.py
+++ b/solution.py
@@ -18,11 +18,34 @@
 GROUP_Y = ("z", "core")
 
 
-def place_in(axes):
-    place = 0
+X_FIRST, Y_FIRST = 15, 0
+Q_FIRST, SECOND_FIRST, PRODUCT_FIRST = 9, 12, 6
+
+
+def index_in(axes):
+    index = 0
     for name in axes:
-        place = place * lax.axis_size(name) + lax.axis_index(name)
-    return place
+        index = index * lax.axis_size(name) + lax.axis_index(name)
+    return index
+
+
+def listed(axes, first):
+    count = math.prod(lax.axis_size(name) for name in axes)
+    if axes == GROUP_Y:
+        return [[(k + first) % count for k in range(count)]]
+    return [[k ^ first for k in range(count)]]
+
+
+def x_place():
+    return jnp.bitwise_xor(index_in(GROUP_X), X_FIRST)
+
+
+def y_place(count):
+    return lax.rem(index_in(GROUP_Y) + count - Y_FIRST, count)
+
+
+def exchanged(x, axes, first):
+    return lax.all_to_all(x, axes, 0, 0, tiled=True, axis_index_groups=listed(axes, first))
 
 
 def three_parts(v):
@@ -104,10 +127,10 @@
         q = q + q_ref[i]
     for i in range(count):
         sum_ref[i] = q[:, i * width : (i + 1) * width]
-    own = sum_ref[place_in(GROUP_X)]
+    own = sum_ref[x_place()]
     inv = 1.0 / q
     pieces = [jnp.broadcast_to(inv[:, t : t + 128], (16, 128)) for t in range(0, total, 128)]
-    mine = place_in(GROUP_Y)
+    mine = y_place(out_ref.shape[0])
     apart = jnp.concatenate(
         [jnp.where(mine == i, 1.0 / own, 0.0) for i in range(k_ref.shape[0] // width)], axis=1
     )
@@ -134,10 +157,10 @@
     count, rows, width = b_ref.shape
     size = rows - out_ref.shape[1]
     lines = k_ref.shape[0] // 128
-    summed = m_ref[0].astype(f32)
-    line_ref[0] = summed
-    for i in range(1, count):
-        lined = m_ref[i].astype(f32)
+    summed = jnp.zeros(m_ref.shape[1:], f32)
+    for k in range(count):
+        i = (k + SECOND_FIRST - Y_FIRST) % count
+        lined = m_ref[k].astype(f32)
         line_ref[i] = lined
         summed = summed + lined * (1.0 / (1.0 + i / count))
     q = jnp.concatenate(
@@ -158,7 +181,7 @@
     weighted = (block * factor).astype(bf16)
     for i in range(count):
         fac_ref[i] = factor[:, i * width : (i + 1) * width]
-    place, mine = place_in(GROUP_X), place_in(GROUP_Y)
+    place, mine = x_place(), y_place(count)
     own = fac_ref[mine]
     own_ref[...] = own
     added = (b_ref[mine, size:] * own).astype(bf16).astype(f32)
@@ -173,7 +196,8 @@
     )
     for i in range(out_ref.shape[0]):
         value = values[:, i * width : (i + 1) * width]
-        out_ref[i] = jnp.where(place == i, value - added, value).astype(bf16)
+        value = jnp.where(place == i, value - added, value)
+        out_ref[i ^ X_FIRST ^ PRODUCT_FIRST] = value.astype(bf16)
 
 
 def per_device(features, block):
@@ -205,8 +229,8 @@
         compiler_params=PARAMS,
         name="spread_block",
     )(*(pltpu.with_memory_space_constraint(a, pltpu.HBM) for a in (features, block)))
-    x_feat = lax.all_to_all(copies, GROUP_X, 0, 0, tiled=True)
-    y_both = lax.all_gather(both, GROUP_Y)
+    x_feat = exchanged(copies, GROUP_X, X_FIRST)
+    y_both = lax.all_gather(both, GROUP_Y, axis_index_groups=listed(GROUP_Y, Y_FIRST))
     kern, q_parts = pl.pallas_call(
         functools.partial(kernel_block, gain),
         out_shape=(
@@ -219,7 +243,7 @@
         compiler_params=PARAMS,
         name="kernel_block",
     )(x_feat, y_both)
-    q_parts = lax.all_to_all(q_parts, GROUP_X, 0, 0, tiled=True)
+    q_parts = exchanged(q_parts, GROUP_X, Q_FIRST)
     sums = pl.pallas_call(
         second_block,
         out_shape=jax.ShapeDtypeStruct((m, lines, 128), bf16),
@@ -229,7 +253,7 @@
         compiler_params=PARAMS,
         name="second_block",
     )(q_parts, kern)
-    sums = lax.all_to_all(sums, GROUP_Y, 0, 0, tiled=True)
+    sums = exchanged(sums, GROUP_Y, SECOND_FIRST)
     parts, factor, diagonal = pl.pallas_call(
         product_block,
         out_shape=(
@@ -243,7 +267,7 @@
         compiler_params=PARAMS,
         name="product_block",
     )(sums, kern, y_both)
-    parts = lax.all_to_all(parts, GROUP_X, 0, 0, tiled=True)
+    parts = exchanged(parts, GROUP_X, PRODUCT_FIRST)
     return (jnp.sum(parts.astype(f32), axis=0) + diagonal) * factor
 
 

time: 71.5 us -> 66.2 us (0.926)
  blocking collectives: 57.4 us -> 50.5 us
  starting transfers between devices: 7.6 us -> 9.18 us
    all_to_all x3, blocking collectives: 35.5 us -> 28.7 us  [exchanged(): lax.all_to_all(x, axes, 0, 0, tiled=True, axis_index_groups=listed(axes,...]
    all_to_all x1, starting transfers between devices: 7.6 us -> 9.18 us  [exchanged(): lax.all_to_all(x, axes, 0, 0, tiled=True, axis_index_groups=listed(axes,...]
where the time goes in v7:
time: 66.2 us; the launch traced here: 65.9 us
  blocking collectives  50.5 us (76%)
  starting transfers between devices  9.18 us (14%)
  Pallas kernels  5.53 us (8%)
    all_to_all x3, blocking collectives, exchanged(): lax.all_to_all(x, axes, 0, 0, tiled=True, axis_index_groups=listed(axes,...  28.7 us
    all_gather x1, blocking collectives, per_device(): lax.all_gather(both, GROUP_Y, axis_index_groups=listed(GROUP_Y, Y_FIRST))  21.8 us
    all_to_all x1, starting transfers between devices, exchanged(): lax.all_to_all(x, axes, 0, 0, tiled=True, axis_index_groups=listed(axes,...  9.18 us
    pallas_call x1, Pallas kernels, per_device(): pl.pallas_call(functools.partial(kernel_block, gain), out_shape=(jax.Shap...  1.98 us
    pallas_call x1, Pallas kernels, per_device(): pl.pallas_call(spread_block, out_shape=(jax.ShapeDtypeStruct((n, width, o...  1.65 us
  transfers between devices with their start and end apart: 1, of which 0 were waited for; matrix products, arithmetic and copies ran while one was open for 0% of the time, Pallas kernels for 0%

profile of v7, /device:TPU:1, one launch (start us, length us, event | category | flops | bytes accessed | tf_op | source)
XLA Modules:
  0.0 65.9 jit_solution(12519501901725594450)
XLA Ops:
  0.0 1.6 %spread_block.1 = (f32[16,32,96]{2,1,0:T(8,128)}, f32[48,96]{1,0:T(8,128)S(1)}) custom-call(f32[32,96]{1,0:T(8,128)} %f_ref.1, f32[16,96]{1,0:T(8,128)} %b_ref.1), custom_call_target="tpu_custom_call" | custom-call | tf_op jit(solution)/shard_map/spread_block/pallas_call | solution.py:214
  1.7 9.2 %all-to-all-start = ((f32[16,32,96]{2,1,0:T(8,128)}), f32[16,32,96]{2,1,0:T(8,128)S(1)}, u32[]{:S(2)}, u32[]{:S(2)}) async-start(f32[16,32,96]{2,1,0:T(8,128)} %get-tuple-element.12), calls=%async_computation | async-start | bytes 524288 | tf_op jit(solution)/shard_map/all_to_all | solution.py:48
  10.8 21.8 %all-gather = f32[768,96]{1,0:T(8,128)S(1)} all-gather(f32[48,96]{1,0:T(8,128)S(1)} %get-tuple-element.13), channel_id=2, replica_groups={{0,1,32,33,64,65,96,97,128,129,160,161,192,193,224,225},{2,3,34,35,66,6..., dimensions={0}, use_global_device_ids=true | all-gather | bytes 313344 | tf_op jit(solution)/shard_map/all_gather | solution.py:233
  32.7 0.0 all-to-all-done.x_ref
  32.7 2.0 %kernel_block.1 = (bf16[1536,1536]{1,0:T(8,128)(2,1)S(1)}, f32[16,1,1536]{2,1,0:T(1,128)S(1)}) custom-call(f32[16,32,96]{2,1,0:T(8,128)S(1)} %all-to-all-done.x_ref, f32[16,48,96]{2,1,0:T(8,128)S(1)} %bitcast.2), custom_call_target="tpu_custom_call" | custom-call | tf_op jit(solution)/shard_map/kernel_block/pallas_call | solution.py:234
  34.7 9.5 %all_to_all.20.q_ref = f32[16,1,1536]{2,1,0:T(1,128)S(1)} all-to-all(f32[16,1,1536]{2,1,0:T(1,128)S(1)} %get-tuple-element.14), channel_id=1, replica_groups={{18,16,22,20,26,24,30,28,2,0,6,4,10,8,14,12},{19,17,23,21,27,25,31,29,3..., dimensions={0} | all-to-all | bytes 196608 | tf_op jit(solution)/shard_map/all_to_all | solution.py:48
  44.1 1.0 %second_block.1 = bf16[16,16,128]{2,1,0:T(8,128)(2,1)S(1)} custom-call(f32[16,1,1536]{2,1,0:T(1,128)S(1)} %all_to_all.20.q_ref, bf16[1536,1536]{1,0:T(8,128)(2,1)S(1)} %get-tuple-element.15.k_ref), custom_call_target="tpu_custom_call" | custom-call | tf_op jit(solution)/shard_map/second_block/pallas_call | solution.py:247
  45.2 10.7 %all_to_all.21.m_ref = bf16[16,16,128]{2,1,0:T(8,128)(2,1)S(1)} all-to-all(bf16[16,16,128]{2,1,0:T(8,128)(2,1)S(1)} %second_block.1), channel_id=1, replica_groups={{192,193,224,225,0,1,32,33,64,65,96,97,128,129,160,161},{194,195,226,22..., dimensions={0} | all-to-all | bytes 131072 | tf_op jit(solution)/shard_map/all_to_all | solution.py:48
  55.9 0.9 %product_block.1 = (bf16[16,16,96]{2,1,0:T(8,128)(2,1)S(1)}, f32[1,96]{1,0:T(1,128)S(1)}, f32[16,96]{1,0:T(8,128)S(1)}) custom-call(bf16[16,16,128]{2,1,0:T(8,128)(2,1)S(1)} %all_to_all.21.m_ref, bf16[1536,1536]{1,0:T(8,128)(2,1)S(1)} %get-tuple-element.15.k_ref, f32[16,48,96]{2,1,0:T(8,128)S(1)} %bitcast.3), custom_call_target="tpu_custom_call" | custom-call | tf_op jit(solution)/shard_map/product_block/pallas_call | solution.py:257
  56.7 8.5 %all_to_all.22 = bf16[16,16,96]{2,1,0:T(8,128)(2,1)S(1)} all-to-all(bf16[16,16,96]{2,1,0:T(8,128)(2,1)S(1)} %get-tuple-element.16), channel_id=1, replica_groups={{12,14,8,10,4,6,0,2,28,30,24,26,20,22,16,18},{13,15,9,11,5,7,1,3,29,31,..., dimensions={0} | all-to-all | bytes 98304 | tf_op jit(solution)/shard_map/all_to_all | solution.py:48
  65.3 0.6 add_multiply_fusion
  (1 shorter events, 0.0 us)
Async XLA Ops:
  1.7 31.0 %all-to-all-start = ((f32[16,32,96]{2,1,0:T(8,128)}), f32[16,32,96]{2,1,0:T(8,128)S(1)}, u32[]{:S(2)}, u32[]{:S(2)}) async-start(f32[16,32,96]{2,1,0:T(8,128)} %get-tuple-element.12), calls=%async_computation | async-start | bytes 524288 | tf_op jit(solution)/shard_map/all_to_all | solution.py:48

commit v8 on v7

--- a/solution.py
+++ b/solution.py
@@ -19,7 +19,7 @@
 
 
 X_FIRST, Y_FIRST = 15, 0
-Q_FIRST, SECOND_FIRST, PRODUCT_FIRST = 9, 12, 6
+Q_FIRST, SECOND_FIRST, PRODUCT_FIRST = 9, 13, 6
 
 
 def index_in(axes):
@@ -72,7 +72,7 @@
     return jnp.concatenate(parts, axis=0)
 
 
-def spread_block(f_ref, b_ref, x_ref, y_ref, here, in_sem, x_sem, y_sem):
+def spread_block(f_ref, b_ref, x_ref, y_ref, here, spread, in_sem, x_sem, y_sem):
     width = f_ref.shape[0]
     fetch = pltpu.make_async_copy(f_ref, here, in_sem)
     fetch.start()
@@ -81,8 +81,13 @@
     lower.start()
     upper.start()
     fetch.wait()
+    values = here[...]
+    for i in range(spread.shape[0]):
+        spread[i] = values
+    share = spread.shape[0]
     copies = [
-        pltpu.make_async_copy(here, x_ref.at[i], x_sem.at[i]) for i in range(x_ref.shape[0])
+        pltpu.make_async_copy(spread, x_ref.at[pl.ds(i * share, share)], x_sem.at[i])
+        for i in range(x_ref.shape[0] // share)
     ]
     for copy in copies:
         copy.start()
@@ -221,8 +226,9 @@
         out_specs=(anywhere,) * 2,
         scratch_shapes=[
             pltpu.VMEM((width, owned), f32),
+            pltpu.VMEM((n // 4, width, owned), f32),
             pltpu.SemaphoreType.DMA,
-            pltpu.SemaphoreType.DMA((n,)),
+            pltpu.SemaphoreType.DMA((4,)),
             pltpu.SemaphoreType.DMA((2,)),
         ],
         cost_estimate=pl.CostEstimate(flops=0, bytes_accessed=0, transcendentals=0),

time: 66.2 us -> 65.9 us (level)
  no operation moved by 1% of the time
where the time goes in v8:
time: 65.9 us; the launch traced here: 65.5 us
  blocking collectives  50.3 us (76%)
  starting transfers between devices  9.18 us (14%)
  Pallas kernels  5.44 us (8%)
    all_to_all x3, blocking collectives, exchanged(): lax.all_to_all(x, axes, 0, 0, tiled=True, axis_index_groups=listed(axes,...  28.4 us
    all_gather x1, blocking collectives, per_device(): lax.all_gather(both, GROUP_Y, axis_index_groups=listed(GROUP_Y, Y_FIRST))  21.8 us
    all_to_all x1, starting transfers between devices, exchanged(): lax.all_to_all(x, axes, 0, 0, tiled=True, axis_index_groups=listed(axes,...  9.18 us
    pallas_call x1, Pallas kernels, per_device(): pl.pallas_call(functools.partial(kernel_block, gain), out_shape=(jax.Shap...  2 us
    pallas_call x1, Pallas kernels, per_device(): pl.pallas_call(spread_block, out_shape=(jax.ShapeDtypeStruct((n, width, o...  1.54 us
  transfers between devices with their start and end apart: 1, of which 0 were waited for; matrix products, arithmetic and copies ran while one was open for 0% of the time, Pallas kernels for 0%

profile of v8, /device:TPU:1, one launch (start us, length us, event | category | flops | bytes accessed | tf_op | source)
XLA Modules:
  0.0 65.5 jit_solution(1767854705657190132)
XLA Ops:
  0.0 1.5 %spread_block.1 = (f32[16,32,96]{2,1,0:T(8,128)}, f32[48,96]{1,0:T(8,128)S(1)}) custom-call(f32[32,96]{1,0:T(8,128)} %f_ref.1, f32[16,96]{1,0:T(8,128)} %b_ref.1), custom_call_target="tpu_custom_call" | custom-call | tf_op jit(solution)/shard_map/spread_block/pallas_call | solution.py:219
  1.6 9.2 %all-to-all-start = ((f32[16,32,96]{2,1,0:T(8,128)}), f32[16,32,96]{2,1,0:T(8,128)S(1)}, u32[]{:S(2)}, u32[]{:S(2)}) async-start(f32[16,32,96]{2,1,0:T(8,128)} %get-tuple-element.12), calls=%async_computation | async-start | bytes 524288 | tf_op jit(solution)/shard_map/all_to_all | solution.py:48
  10.7 21.8 %all-gather = f32[768,96]{1,0:T(8,128)S(1)} all-gather(f32[48,96]{1,0:T(8,128)S(1)} %get-tuple-element.13), channel_id=2, replica_groups={{0,1,32,33,64,65,96,97,128,129,160,161,192,193,224,225},{2,3,34,35,66,6..., dimensions={0}, use_global_device_ids=true | all-gather | bytes 313344 | tf_op jit(solution)/shard_map/all_gather | solution.py:239
  32.6 0.0 all-to-all-done.x_ref
  32.6 2.0 %kernel_block.1 = (bf16[1536,1536]{1,0:T(8,128)(2,1)S(1)}, f32[16,1,1536]{2,1,0:T(1,128)S(1)}) custom-call(f32[16,32,96]{2,1,0:T(8,128)S(1)} %all-to-all-done.x_ref, f32[16,48,96]{2,1,0:T(8,128)S(1)} %bitcast.2), custom_call_target="tpu_custom_call" | custom-call | tf_op jit(solution)/shard_map/kernel_block/pallas_call | solution.py:240
  34.6 9.5 %all_to_all.20.q_ref = f32[16,1,1536]{2,1,0:T(1,128)S(1)} all-to-all(f32[16,1,1536]{2,1,0:T(1,128)S(1)} %get-tuple-element.14), channel_id=1, replica_groups={{18,16,22,20,26,24,30,28,2,0,6,4,10,8,14,12},{19,17,23,21,27,25,31,29,3..., dimensions={0} | all-to-all | bytes 196608 | tf_op jit(solution)/shard_map/all_to_all | solution.py:48
  44.0 1.0 %second_block.1 = bf16[16,16,128]{2,1,0:T(8,128)(2,1)S(1)} custom-call(f32[16,1,1536]{2,1,0:T(1,128)S(1)} %all_to_all.20.q_ref, bf16[1536,1536]{1,0:T(8,128)(2,1)S(1)} %get-tuple-element.15.k_ref), custom_call_target="tpu_custom_call" | custom-call | tf_op jit(solution)/shard_map/second_block/pallas_call | solution.py:253
  45.1 10.4 %all_to_all.21.m_ref = bf16[16,16,128]{2,1,0:T(8,128)(2,1)S(1)} all-to-all(bf16[16,16,128]{2,1,0:T(8,128)(2,1)S(1)} %second_block.1), channel_id=1, replica_groups={{193,224,225,0,1,32,33,64,65,96,97,128,129,160,161,192},{195,226,227,2,..., dimensions={0} | all-to-all | bytes 131072 | tf_op jit(solution)/shard_map/all_to_all | solution.py:48
  55.5 0.9 %product_block.1 = (bf16[16,16,96]{2,1,0:T(8,128)(2,1)S(1)}, f32[1,96]{1,0:T(1,128)S(1)}, f32[16,96]{1,0:T(8,128)S(1)}) custom-call(bf16[16,16,128]{2,1,0:T(8,128)(2,1)S(1)} %all_to_all.21.m_ref, bf16[1536,1536]{1,0:T(8,128)(2,1)S(1)} %get-tuple-element.15.k_ref, f32[16,48,96]{2,1,0:T(8,128)S(1)} %bitcast.3), custom_call_target="tpu_custom_call" | custom-call | tf_op jit(solution)/shard_map/product_block/pallas_call | solution.py:263
  56.4 8.5 %all_to_all.22 = bf16[16,16,96]{2,1,0:T(8,128)(2,1)S(1)} all-to-all(bf16[16,16,96]{2,1,0:T(8,128)(2,1)S(1)} %get-tuple-element.16), channel_id=1, replica_groups={{12,14,8,10,4,6,0,2,28,30,24,26,20,22,16,18},{13,15,9,11,5,7,1,3,29,31,..., dimensions={0} | all-to-all | bytes 98304 | tf_op jit(solution)/shard_map/all_to_all | solution.py:48
  64.9 0.6 add_multiply_fusion
  (1 shorter events, 0.0 us)
Async XLA Ops:
  1.6 31.0 %all-to-all-start = ((f32[16,32,96]{2,1,0:T(8,128)}), f32[16,32,96]{2,1,0:T(8,128)S(1)}, u32[]{:S(2)}, u32[]{:S(2)}) async-start(f32[16,32,96]{2,1,0:T(8,128)} %get-tuple-element.12), calls=%async_computation | async-start | bytes 524288 | tf_op jit(solution)/shard_map/all_to_all | solution.py:48

commit v9 on v8

--- a/solution.py
+++ b/solution.py
@@ -104,18 +104,21 @@
     right_ref[...] = extended(x, False)
     step = 512
     sums = [jnp.zeros((8, step), f32) for _ in range(0, total, step)]
-    for i in range(y_ref.shape[0]):
-        left = extended(y_ref[i, :size] * gain, True)
+    group = math.gcd(4, y_ref.shape[0])
+    tall = group * width
+    for i in range(0, y_ref.shape[0], group):
+        y = jnp.concatenate([y_ref[i + k, :size] for k in range(group)], axis=1) * gain
+        left = extended(y, True)
         for j in range(0, total, step):
             expo = lax.dot_general(
                 left, right_ref[:, j : j + step], (((0,), (0,)), ((), ())),
                 preferred_element_type=f32,
             )
             tile = jnp.exp2(expo).astype(bf16)
-            k_ref[i * width : (i + 1) * width, j : j + step] = tile
+            k_ref[i * width : i * width + tall, j : j + step] = tile
             wide = tile.astype(f32)
             part = sums[j // step]
-            for r in range(0, width, 8):
+            for r in range(0, tall, 8):
                 part = part + wide[r : r + 8]
             sums[j // step] = part
     flat = jnp.sum(jnp.concatenate(sums, axis=1), axis=0, keepdims=True)

time: 65.9 us -> 65.8 us (level)
  no operation moved by 1% of the time
where the time goes in v9:
time: 65.8 us; the launch traced here: 65.5 us
  blocking collectives  50.3 us (76%)
  starting transfers between devices  9.18 us (14%)
  Pallas kernels  5.41 us (8%)
    all_to_all x3, blocking collectives, exchanged(): lax.all_to_all(x, axes, 0, 0, tiled=True, axis_index_groups=listed(axes,...  28.4 us
    all_gather x1, blocking collectives, per_device(): lax.all_gather(both, GROUP_Y, axis_index_groups=listed(GROUP_Y, Y_FIRST))  21.8 us
    all_to_all x1, starting transfers between devices, exchanged(): lax.all_to_all(x, axes, 0, 0, tiled=True, axis_index_groups=listed(axes,...  9.18 us
    pallas_call x1, Pallas kernels, per_device(): pl.pallas_call(functools.partial(kernel_block, gain), out_shape=(jax.Shap...  1.96 us
    pallas_call x1, Pallas kernels, per_device(): pl.pallas_call(spread_block, out_shape=(jax.ShapeDtypeStruct((n, width, o...  1.54 us
  transfers between devices with their start and end apart: 1, of which 0 were waited for; matrix products, arithmetic and copies ran while one was open for 0% of the time, Pallas kernels for 0%

profile of v9, /device:TPU:1, one launch (start us, length us, event | category | flops | bytes accessed | tf_op | source)
XLA Modules:
  0.0 65.5 jit_solution(12451926684063607453)
XLA Ops:
  0.0 1.5 %spread_block.1 = (f32[16,32,96]{2,1,0:T(8,128)}, f32[48,96]{1,0:T(8,128)S(1)}) custom-call(f32[32,96]{1,0:T(8,128)} %f_ref.1, f32[16,96]{1,0:T(8,128)} %b_ref.1), custom_call_target="tpu_custom_call" | custom-call | tf_op jit(solution)/shard_map/spread_block/pallas_call | solution.py:222
  1.6 9.2 %all-to-all-start = ((f32[16,32,96]{2,1,0:T(8,128)}), f32[16,32,96]{2,1,0:T(8,128)S(1)}, u32[]{:S(2)}, u32[]{:S(2)}) async-start(f32[16,32,96]{2,1,0:T(8,128)} %get-tuple-element.12), calls=%async_computation | async-start | bytes 524288 | tf_op jit(solution)/shard_map/all_to_all | solution.py:48
  10.7 21.8 %all-gather = f32[768,96]{1,0:T(8,128)S(1)} all-gather(f32[48,96]{1,0:T(8,128)S(1)} %get-tuple-element.13), channel_id=2, replica_groups={{0,1,32,33,64,65,96,97,128,129,160,161,192,193,224,225},{2,3,34,35,66,6..., dimensions={0}, use_global_device_ids=true | all-gather | bytes 313344 | tf_op jit(solution)/shard_map/all_gather | solution.py:242
  32.6 0.0 all-to-all-done.x_ref
  32.6 2.0 %kernel_block.1 = (bf16[1536,1536]{1,0:T(8,128)(2,1)S(1)}, f32[16,1,1536]{2,1,0:T(1,128)S(1)}) custom-call(f32[16,32,96]{2,1,0:T(8,128)S(1)} %all-to-all-done.x_ref, f32[16,48,96]{2,1,0:T(8,128)S(1)} %bitcast.2), custom_call_target="tpu_custom_call" | custom-call | tf_op jit(solution)/shard_map/kernel_block/pallas_call | solution.py:243
  34.5 9.5 %all_to_all.20.q_ref = f32[16,1,1536]{2,1,0:T(1,128)S(1)} all-to-all(f32[16,1,1536]{2,1,0:T(1,128)S(1)} %get-tuple-element.14), channel_id=1, replica_groups={{18,16,22,20,26,24,30,28,2,0,6,4,10,8,14,12},{19,17,23,21,27,25,31,29,3..., dimensions={0} | all-to-all | bytes 196608 | tf_op jit(solution)/shard_map/all_to_all | solution.py:48
  44.0 1.0 %second_block.1 = bf16[16,16,128]{2,1,0:T(8,128)(2,1)S(1)} custom-call(f32[16,1,1536]{2,1,0:T(1,128)S(1)} %all_to_all.20.q_ref, bf16[1536,1536]{1,0:T(8,128)(2,1)S(1)} %get-tuple-element.15.k_ref), custom_call_target="tpu_custom_call" | custom-call | tf_op jit(solution)/shard_map/second_block/pallas_call | solution.py:256
  45.0 10.4 %all_to_all.21.m_ref = bf16[16,16,128]{2,1,0:T(8,128)(2,1)S(1)} all-to-all(bf16[16,16,128]{2,1,0:T(8,128)(2,1)S(1)} %second_block.1), channel_id=1, replica_groups={{193,224,225,0,1,32,33,64,65,96,97,128,129,160,161,192},{195,226,227,2,..., dimensions={0} | all-to-all | bytes 131072 | tf_op jit(solution)/shard_map/all_to_all | solution.py:48
  55.5 0.9 %product_block.1 = (bf16[16,16,96]{2,1,0:T(8,128)(2,1)S(1)}, f32[1,96]{1,0:T(1,128)S(1)}, f32[16,96]{1,0:T(8,128)S(1)}) custom-call(bf16[16,16,128]{2,1,0:T(8,128)(2,1)S(1)} %all_to_all.21.m_ref, bf16[1536,1536]{1,0:T(8,128)(2,1)S(1)} %get-tuple-element.15.k_ref, f32[16,48,96]{2,1,0:T(8,128)S(1)} %bitcast.3), custom_call_target="tpu_custom_call" | custom-call | tf_op jit(solution)/shard_map/product_block/pallas_call | solution.py:266
  56.3 8.5 %all_to_all.22 = bf16[16,16,96]{2,1,0:T(8,128)(2,1)S(1)} all-to-all(bf16[16,16,96]{2,1,0:T(8,128)(2,1)S(1)} %get-tuple-element.16), channel_id=1, replica_groups={{12,14,8,10,4,6,0,2,28,30,24,26,20,22,16,18},{13,15,9,11,5,7,1,3,29,31,..., dimensions={0} | all-to-all | bytes 98304 | tf_op jit(solution)/shard_map/all_to_all | solution.py:48
  64.9 0.6 add_multiply_fusion
  (1 shorter events, 0.0 us)
Async XLA Ops:
  1.6 31.0 %all-to-all-start = ((f32[16,32,96]{2,1,0:T(8,128)}), f32[16,32,96]{2,1,0:T(8,128)S(1)}, u32[]{:S(2)}, u32[]{:S(2)}) async-start(f32[16,32,96]{2,1,0:T(8,128)} %get-tuple-element.12), calls=%async_computation | async-start | bytes 524288 | tf_op jit(solution)/shard_map/all_to_all | solution.py:48

commit v10 on v9

--- a/solution.py
+++ b/solution.py
@@ -19,7 +19,7 @@
 
 
 X_FIRST, Y_FIRST = 15, 0
-Q_FIRST, SECOND_FIRST, PRODUCT_FIRST = 9, 13, 6
+Q_FIRST, SECOND_FIRST, PRODUCT_FIRST = 9, 11, 6
 
 
 def index_in(axes):

time: 65.8 us -> 65.9 us (level)
  no operation moved by 1% of the time
where the time goes in v10:
time: 65.9 us; the launch traced here: 65.6 us
  blocking collectives  50.3 us (76%)
  starting transfers between devices  9.18 us (14%)
  Pallas kernels  5.41 us (8%)
    all_to_all x3, blocking collectives, exchanged(): lax.all_to_all(x, axes, 0, 0, tiled=True, axis_index_groups=listed(axes,...  28.5 us
    all_gather x1, blocking collectives, per_device(): lax.all_gather(both, GROUP_Y, axis_index_groups=listed(GROUP_Y, Y_FIRST))  21.8 us
    all_to_all x1, starting transfers between devices, exchanged(): lax.all_to_all(x, axes, 0, 0, tiled=True, axis_index_groups=listed(axes,...  9.18 us
    pallas_call x1, Pallas kernels, per_device(): pl.pallas_call(functools.partial(kernel_block, gain), out_shape=(jax.Shap...  1.96 us
    pallas_call x1, Pallas kernels, per_device(): pl.pallas_call(spread_block, out_shape=(jax.ShapeDtypeStruct((n, width, o...  1.54 us
  transfers between devices with their start and end apart: 1, of which 0 were waited for; matrix products, arithmetic and copies ran while one was open for 0% of the time, Pallas kernels for 0%

profile of v10, /device:TPU:1, one launch (start us, length us, event | category | flops | bytes accessed | tf_op | source)
XLA Modules:
  0.0 65.6 jit_solution(5769798441104140904)
XLA Ops:
  0.0 1.5 %spread_block.1 = (f32[16,32,96]{2,1,0:T(8,128)}, f32[48,96]{1,0:T(8,128)S(1)}) custom-call(f32[32,96]{1,0:T(8,128)} %f_ref.1, f32[16,96]{1,0:T(8,128)} %b_ref.1), custom_call_target="tpu_custom_call" | custom-call | tf_op jit(solution)/shard_map/spread_block/pallas_call | solution.py:222
  1.6 9.2 %all-to-all-start = ((f32[16,32,96]{2,1,0:T(8,128)}), f32[16,32,96]{2,1,0:T(8,128)S(1)}, u32[]{:S(2)}, u32[]{:S(2)}) async-start(f32[16,32,96]{2,1,0:T(8,128)} %get-tuple-element.12), calls=%async_computation | async-start | bytes 524288 | tf_op jit(solution)/shard_map/all_to_all | solution.py:48
  10.7 21.8 %all-gather = f32[768,96]{1,0:T(8,128)S(1)} all-gather(f32[48,96]{1,0:T(8,128)S(1)} %get-tuple-element.13), channel_id=2, replica_groups={{0,1,32,33,64,65,96,97,128,129,160,161,192,193,224,225},{2,3,34,35,66,6..., dimensions={0}, use_global_device_ids=true | all-gather | bytes 313344 | tf_op jit(solution)/shard_map/all_gather | solution.py:242
  32.6 0.0 all-to-all-done.x_ref
  32.6 2.0 %kernel_block.1 = (bf16[1536,1536]{1,0:T(8,128)(2,1)S(1)}, f32[16,1,1536]{2,1,0:T(1,128)S(1)}) custom-call(f32[16,32,96]{2,1,0:T(8,128)S(1)} %all-to-all-done.x_ref, f32[16,48,96]{2,1,0:T(8,128)S(1)} %bitcast.2), custom_call_target="tpu_custom_call" | custom-call | tf_op jit(solution)/shard_map/kernel_block/pallas_call | solution.py:243
  34.5 9.5 %all_to_all.20.q_ref = f32[16,1,1536]{2,1,0:T(1,128)S(1)} all-to-all(f32[16,1,1536]{2,1,0:T(1,128)S(1)} %get-tuple-element.14), channel_id=1, replica_groups={{18,16,22,20,26,24,30,28,2,0,6,4,10,8,14,12},{19,17,23,21,27,25,31,29,3..., dimensions={0} | all-to-all | bytes 196608 | tf_op jit(solution)/shard_map/all_to_all | solution.py:48
  44.0 1.0 %second_block.1 = bf16[16,16,128]{2,1,0:T(8,128)(2,1)S(1)} custom-call(f32[16,1,1536]{2,1,0:T(1,128)S(1)} %all_to_all.20.q_ref, bf16[1536,1536]{1,0:T(8,128)(2,1)S(1)} %get-tuple-element.15.k_ref), custom_call_target="tpu_custom_call" | custom-call | tf_op jit(solution)/shard_map/second_block/pallas_call | solution.py:256
  45.0 10.5 %all_to_all.21.m_ref = bf16[16,16,128]{2,1,0:T(8,128)(2,1)S(1)} all-to-all(bf16[16,16,128]{2,1,0:T(8,128)(2,1)S(1)} %second_block.1), channel_id=1, replica_groups={{161,192,193,224,225,0,1,32,33,64,65,96,97,128,129,160},{163,194,195,22..., dimensions={0} | all-to-all | bytes 131072 | tf_op jit(solution)/shard_map/all_to_all | solution.py:48
  55.5 0.9 %product_block.1 = (bf16[16,16,96]{2,1,0:T(8,128)(2,1)S(1)}, f32[1,96]{1,0:T(1,128)S(1)}, f32[16,96]{1,0:T(8,128)S(1)}) custom-call(bf16[16,16,128]{2,1,0:T(8,128)(2,1)S(1)} %all_to_all.21.m_ref, bf16[1536,1536]{1,0:T(8,128)(2,1)S(1)} %get-tuple-element.15.k_ref, f32[16,48,96]{2,1,0:T(8,128)S(1)} %bitcast.3), custom_call_target="tpu_custom_call" | custom-call | tf_op jit(solution)/shard_map/product_block/pallas_call | solution.py:266
  56.4 8.5 %all_to_all.22 = bf16[16,16,96]{2,1,0:T(8,128)(2,1)S(1)} all-to-all(bf16[16,16,96]{2,1,0:T(8,128)(2,1)S(1)} %get-tuple-element.16), channel_id=1, replica_groups={{12,14,8,10,4,6,0,2,28,30,24,26,20,22,16,18},{13,15,9,11,5,7,1,3,29,31,..., dimensions={0} | all-to-all | bytes 98304 | tf_op jit(solution)/shard_map/all_to_all | solution.py:48
  65.0 0.6 add_multiply_fusion
  (1 shorter events, 0.0 us)
Async XLA Ops:
  1.6 31.0 %all-to-all-start = ((f32[16,32,96]{2,1,0:T(8,128)}), f32[16,32,96]{2,1,0:T(8,128)S(1)}, u32[]{:S(2)}, u32[]{:S(2)}) async-start(f32[16,32,96]{2,1,0:T(8,128)} %get-tuple-element.12), calls=%async_computation | async-start | bytes 524288 | tf_op jit(solution)/shard_map/all_to_all | solution.py:48
